TPU v7x, 32 devices: a whole 2x2x4 slice. The times are simulated.
32 devices in a mesh: blk: 16 (over z, y, core), ffn: 2 (over x).
Axes of the slice: x: 2, y: 2, z: 4, core: 2. Of those that a mesh axis runs over, the one named last changes fastest.
Arguments:
- tokens: bfloat16 [4096, 4608], P('blk'), may hold values from -6 to 6
- ln_gain: float32 [4608], replicated, may hold values from 0.5 to 2
- ln_bias: float32 [4608], replicated, may hold values from -3 to 3
- fc1_tiles: bfloat16 [16, 2, 101, 128, 128], P('blk', 'ffn'), may hold values from -0.125 to 0.125
- fc1_index: int32 [16, 2, 101], P('blk', 'ffn'), may hold values from 0 to 2591, as said below
- fc1_count: int32 [16, 2], P('blk', 'ffn'), may hold values from 60 to 101, as said below
- fc1_bias: float32 [18432], P('ffn'), may hold values from -3 to 3
- fc2_tiles: bfloat16 [16, 2, 101, 128, 128], P('blk', 'ffn'), may hold values from -0.09375 to 0.09375
- fc2_index: int32 [16, 2, 101], P('blk', 'ffn'), may hold values from 0 to 2591, as said below
- fc2_count: int32 [16, 2], P('blk', 'ffn'), may hold values from 60 to 101, as said below
- fc2_bias: float32 [4608], P('ffn'), may hold values from -3 to 3
Outputs:
- result: bfloat16 [4096, 4608], P('blk', 'ffn')
Inputs may be any that keep to these rules, and one draw needn't show every extreme that they name: `fc1_index`: within one index f of ffn, the positions of all live slots (s < the shard's count) are distinct. `fc2_index`: as for fc1_index. `fc1_count`: some shard of every index of ffn has all 101 slots live. `fc2_count`: as for fc1_count.
All inputs are finite; a program needn't handle non-finite values.
Results may differ from a plain program's by a relative error of at most 0.01.
Values may be sent and summed in bfloat16 or wider, within the bound.
No kernel may reach another device: no remote copies, remote signals or barrier semaphores. Data moves between devices by JAX's collectives and lax.ppermute only.
A program may use at most 256 MiB of HBM per device.

v0:
```python
import functools

import jax
import jax.numpy as jnp
from jax import lax
from jax.experimental import pallas as pl
from jax.experimental.pallas import tpu as pltpu
from jax.sharding import PartitionSpec as P

UNROLL = 4
VMEM_BYTES = 56 * 1024 * 1024
LAST_VMEM_BYTES = 36 * 1024 * 1024


def group_kernel(group, size, zero_row, row_ref, col_ref, field_ref, count_ref, fill_ref, open_ref):
    step, steps = pl.program_id(0), pl.num_programs(0)
    listed = row_ref.shape[0] // steps

    def field(number, at):
        return (number * steps + step) * size + at

    def clear(at, carry):
        field_ref[field(0, at)] = 0
        for g in range(group):
            field_ref[field(1 + g, at)] = 0
            field_ref[field(1 + group + g, at)] = zero_row
        return carry

    def no_group(c, carry):
        fill_ref[c] = 0
        open_ref[c] = 0
        return carry

    def place(tile, groups):
        col = col_ref[step * listed + tile]
        held = jnp.maximum(col, 0)
        filled = fill_ref[held]
        opens = (col >= 0) & (filled == 0)
        at = jnp.where(opens, groups, open_ref[held])

        @pl.when(col >= 0)
        def _():
            open_ref[held] = at
            fill_ref[held] = jnp.where(filled == group - 1, 0, filled + 1)
            field_ref[field(0, at)] = col
            field_ref[field(1 + filled, at)] = tile
            field_ref[field(1 + group + filled, at)] = row_ref[step * listed + tile]

        return groups + opens.astype(jnp.int32)

    lax.fori_loop(0, size, clear, 0)
    lax.fori_loop(0, fill_ref.shape[0], no_group, 0)
    count_ref[step] = lax.fori_loop(0, listed, place, jnp.int32(0))


def group_up(rows, cols, live, blocks, zero_row, group):
    steps, listed = rows.shape
    most = (listed + (group - 1) * min(blocks, listed)) // group
    size = -(-most // UNROLL) * UNROLL
    smem = pl.BlockSpec(memory_space=pltpu.SMEM)
    return pl.pallas_call(
        functools.partial(group_kernel, group, size, zero_row),
        out_shape=[
            jax.ShapeDtypeStruct(((2 * group + 1) * steps * size,), jnp.int32),
            jax.ShapeDtypeStruct((steps,), jnp.int32),
        ],
        grid=(steps,),
        in_specs=[smem, smem],
        out_specs=[smem, smem],
        scratch_shapes=[pltpu.SMEM((blocks,), jnp.int32), pltpu.SMEM((blocks,), jnp.int32)],
        cost_estimate=pl.CostEstimate(flops=0, bytes_accessed=16 * steps * listed, transcendentals=0),
    )(rows.reshape(-1), jnp.where(live, cols, -1).reshape(-1))


def add_block(field_ref, count_ref, x_ref, w_ref, acc, group):
    step, steps = pl.program_id(0), pl.num_programs(0)
    w_ref = w_ref.reshape(-1, *w_ref.shape[2:])
    fields = 2 * group + 1
    size = field_ref.shape[0] // (fields * steps)

    def one(at):
        col, *parts = (field_ref[(f * steps + step) * size + at] for f in range(fields))
        left = jnp.concatenate([x_ref[row] for row in parts[group:]], axis=1)
        right = jnp.concatenate([w_ref[tile] for tile in parts[:group]], axis=0)
        acc[col] += jnp.dot(left, right, preferred_element_type=jnp.float32)

    def several(turn, carry):
        for u in range(UNROLL):
            one(turn * UNROLL + u)
        return carry

    lax.fori_loop(0, lax.div(count_ref[step] + UNROLL - 1, jnp.int32(UNROLL)), several, 0)


def for_blocks(count, work):
    def turn(c, carry):
        work(c)
        return carry

    lax.fori_loop(0, count, turn, 0)


def columns(c, width):
    return pl.ds(pl.multiple_of(c * width, width), width)


def at_start(work):
    pl.when(pl.program_id(0) == 0)(work)


def at_end(work):
    pl.when(pl.program_id(0) == pl.num_programs(0) - 1)(work)


def first_kernel(group, field_ref, count_ref, at_ref, x_ref, w_ref, bias_ref, sum_ref):
    @at_start
    def _():
        def fill(c):
            sum_ref[c] = jnp.broadcast_to(bias_ref[c], sum_ref.shape[1:])

        for_blocks(sum_ref.shape[0], fill)

    add_block(field_ref, count_ref, x_ref, w_ref, sum_ref, group)


def hidden_kernel(group, field_ref, count_ref, at_ref, x_ref, w_ref, sum_ref, out_ref, acc):
    blocks = acc.shape[0]

    @at_start
    def _():
        def fill(c):
            acc[c] = sum_ref[c]

        for_blocks(blocks, fill)

    add_block(field_ref, count_ref, x_ref, w_ref, acc, group)

    @at_end
    def _():
        def finish(c):
            out_ref[c] = jnp.maximum(acc[c], 0.0).astype(out_ref.dtype)

        for_blocks(blocks, finish)
        out_ref[blocks] = jnp.zeros(out_ref.shape[1:], out_ref.dtype)


def partial_kernel(group, field_ref, count_ref, at_ref, x_ref, w_ref, sum_ref, out_ref):
    blocks, width = sum_ref.shape[0], sum_ref.shape[2]

    @at_start
    def _():
        def fill(c):
            sum_ref[c] = jnp.zeros(sum_ref.shape[1:], sum_ref.dtype)

        for_blocks(blocks, fill)

    add_block(field_ref, count_ref, x_ref, w_ref, sum_ref, group)

    @at_end
    def _():
        def finish(c):
            out_ref[:, columns(c, width)] = sum_ref[c].astype(out_ref.dtype)

        for_blocks(blocks, finish)


def result_kernel(
    group, field_ref, count_ref, at_ref,
    x_ref, w_ref, sum_ref, token_ref, other_ref, bias_ref, out_ref, acc,
):
    blocks, width = acc.shape[0], acc.shape[2]

    @at_start
    def _():
        def fill(c):
            acc[c] = sum_ref[c]

        for_blocks(blocks, fill)

    add_block(field_ref, count_ref, x_ref, w_ref, acc, group)

    @at_end
    def _():
        def finish(c):
            cols = columns(c, width)
            value = token_ref[:, cols].astype(jnp.float32) + (acc[c] + other_ref[:, cols])
            out_ref[:, cols] = (value + bias_ref[:, cols]).astype(out_ref.dtype)

        for_blocks(blocks, finish)


def fixed(shape):
    return pl.BlockSpec(shape, lambda i, *_: (0,) * len(shape), pipeline_mode=pl.Buffered(1))


def planned(rows, cols, live, blocks, zero_row, steps, group):
    steps = steps if rows.shape[0] % steps == 0 else 1
    return group_up(*(v.reshape(steps, -1) for v in (rows, cols, live)), blocks, zero_row, group)


def tile_pass(
    kernel, rows, cols, live, at, x, tiles, more, more_specs, out_shapes, blocks,
    steps=4, group=2, scratch=True, vmem=VMEM_BYTES, plan=None,
):
    shards, slots = rows.shape
    side, tokens = tiles.shape[-1], x.shape[1]
    steps = steps if shards % steps == 0 else 1
    if plan is None:
        plan = planned(rows, cols, live, blocks, x.shape[0] - 1, steps, group)
    fields, counts = plan
    return pl.pallas_call(
        functools.partial(kernel, group),
        out_shape=out_shapes,
        grid_spec=pltpu.PrefetchScalarGridSpec(
            num_scalar_prefetch=3,
            grid=(steps,),
            in_specs=[
                fixed(x.shape),
                pl.BlockSpec((shards // steps, slots, side, side), lambda i, *_: (i, 0, 0, 0)),
                *more_specs,
            ],
            out_specs=[
                pl.BlockSpec(o.shape, lambda i, *_, rank=len(o.shape): (0,) * rank) for o in out_shapes
            ],
            scratch_shapes=[pltpu.VMEM((blocks, tokens, side), jnp.float32)] if scratch else [],
        ),
        compiler_params=pltpu.CompilerParams(vmem_limit_bytes=vmem),
        cost_estimate=pl.CostEstimate(
            flops=4 * shards * slots * tokens * side * side,
            bytes_accessed=shards * slots * side * side * 2,
            transcendentals=0,
        ),
    )(fields, counts, at.reshape(1), x, tiles, *more)


def layout_kernel(
    levels, capacity, index_ref, own_ref, count_ref, left_ref, at_ref,
    code_ref, front_count_ref, length_ref, order_ref, send_ref,
    place_ref, source_ref, fronts, backs, sent_ref,
):
    shards = count_ref.shape[0]
    slots = index_ref.shape[0] // shards
    total = order_ref.shape[0]
    me = at_ref[0]

    def times(count, work):
        def turn(i, carry):
            work(i)
            return carry

        lax.fori_loop(0, count, turn, 0)

    def spot(back, shard, i):
        return (back * shards + shard) * capacity + i

    def build(shard):
        left = left_ref[shard]

        def first(i):
            place_ref[spot(0, shard, i)] = 0
            source_ref[spot(0, shard, i)] = i

        def second(slot, carry):
            front, back = carry
            own = own_ref[shard * slots + slot]
            at = spot(own, shard, jnp.where(own == 1, back, front))
            place_ref[at] = index_ref[shard * slots + slot]
            source_ref[at] = capacity - slots + slot
            return front + 1 - own, back + own

        times(left, first)
        fronts[shard], backs[shard] = lax.fori_loop(0, count_ref[shard], second, (left, jnp.int32(0)))

    def even(back, stride, most, so_far, send_at):
        numbers = backs if back else fronts

        def weight(shard):
            return fronts[shard] + backs[shard] if back else fronts[shard]

        def decide(shard):
            partner = shard ^ stride
            excess = lax.div(jnp.maximum(weight(shard) - weight(partner), 0), jnp.int32(2))
            spare = numbers[shard] if back else numbers[shard] - left_ref[shard]
            room = jnp.minimum(most, capacity - numbers[partner])
            sent_ref[shard] = jnp.minimum(excess, jnp.minimum(room, spare))

        def hand_over(shard):
            partner, sent = shard ^ stride, sent_ref[shard]
            here, there = numbers[shard] - sent, numbers[partner]

            def one(i):
                old, new = spot(back, shard, here + i), spot(back, partner, there + i)
                place_ref[new] = place_ref[old]

                @pl.when(shard == me)
                def _():
                    send_ref[send_at + i] = source_ref[old]

                source_ref[new] = so_far + i

            times(sent, one)

        def settle(shard):
            numbers[shard] = numbers[shard] - sent_ref[shard] + sent_ref[shard ^ stride]

        for work in (decide, hand_over, settle):
            times(shards, work)

    def lay_out(shard):
        front, back = fronts[shard], backs[shard]
        front_count_ref[shard] = front
        length_ref[shard] = front + back

        def copy(back, start):
            def one(i):
                code_ref[shard * total + start + i] = place_ref[spot(back, shard, i)]

                @pl.when(shard == me)
                def _():
                    order_ref[start + i] = source_ref[spot(back, shard, i)]

            return one

        times(front, copy(0, 0))
        times(back, copy(1, front))

    def clear(ref):
        def one(i):
            ref[i] = 0

        times(ref.shape[0], one)

    clear(order_ref)
    clear(send_ref)
    times(shards, build)
    so_far, send_at = capacity, 0
    for stride, most_front, most_back in levels:
        for back, most in ((0, most_front), (1, most_back)):
            if most:
                even(back, stride, most, so_far, send_at)
            so_far, send_at = so_far + most, send_at + most
    times(shards, lay_out)


def laid_out(levels, capacity, total, index, own, count, left, blk):
    shards, slots = index.shape
    smem = pl.BlockSpec(memory_space=pltpu.SMEM)
    sizes = [shards * total, shards, shards, total, sum(front + back for _, front, back in levels)]
    scratch = [2 * shards * capacity, 2 * shards * capacity, shards, shards, shards]
    return pl.pallas_call(
        functools.partial(layout_kernel, levels, capacity),
        out_shape=[jax.ShapeDtypeStruct((size,), jnp.int32) for size in sizes],
        in_specs=[smem] * 5,
        out_specs=[smem] * 5,
        scratch_shapes=[pltpu.SMEM((size,), jnp.int32) for size in scratch],
        cost_estimate=pl.CostEstimate(flops=0, bytes_accessed=16 * shards * slots, transcendentals=0),
    )(index.reshape(-1), own.reshape(-1), count, left, blk.reshape(1))


def on_device(
    tokens,
    ln_gain,
    ln_bias,
    fc1_tiles,
    fc1_index,
    fc1_count,
    fc1_bias,
    fc2_tiles,
    fc2_index,
    fc2_count,
    fc2_bias,
    ffn_size,
):
    side = fc1_tiles.shape[-1]
    slots = fc1_tiles.shape[2]
    shards = lax.axis_size("blk")
    token_rows, width = tokens.shape
    first_blocks = fc1_bias.shape[0] // side
    second_blocks = width // side
    share = width // ffn_size
    blk, ffn = lax.axis_index("blk"), lax.axis_index("ffn")
    aligned = share % side == 0
    opening = slots * 5 // 7
    rest = slots - opening
    held = slots + slots // 100
    late_from = held - slots // 3
    levels = [
        (stride, slots // most, max(slots // least, 1))
        for stride, most, least in ((1, 6, 8), (2, 16, 16), (4, 32, 16), (8, slots + 1, 16))
        if shards % (2 * stride) == 0
    ]
    slot_ids = jnp.arange(slots, dtype=jnp.int32)

    def gathered(value):
        return lax.all_gather(value, "blk", axis=0, tiled=True).reshape(shards, -1, side, side)

    tiles1 = gathered(fc1_tiles[0, 0, :opening])
    meta = jnp.concatenate([fc1_index[:, 0], fc2_index[:, 0], fc1_count, fc2_count], axis=1)
    meta = lax.all_gather(meta, "blk", axis=0, tiled=True)
    index1, index2 = meta[:, :slots], meta[:, slots : 2 * slots]
    count1, count2 = meta[:, 2 * slots], meta[:, 2 * slots + 1]
    left1 = jnp.maximum(count1 - opening, 0)

    def in_own_share(index):
        if not aligned:
            return jnp.zeros(index.shape, jnp.bool_)
        return index % second_blocks // (share // side) == ffn

    capacity = rest + slots
    total_ids = jnp.arange(2 * capacity + slots // 4, dtype=jnp.int32)
    codes, fronts, lengths, order, sends = laid_out(
        levels, capacity, total_ids.shape[0], index2, in_own_share(index2).astype(jnp.int32), count2, left1, blk
    )
    codes = codes.reshape(shards, -1)
    sources = jnp.concatenate([fc1_tiles[0, 0, opening:], fc2_tiles[0, 0]], axis=0)
    for stride, most_front, most_back in levels:
        sending, sends = sends[: most_front + most_back], sends[most_front + most_back :]
        arrived = lax.ppermute(
            jnp.take(sources, sending, axis=0, mode="clip"),
            "blk",
            [(i, i ^ stride) for i in range(shards)],
        )
        sources = jnp.concatenate([sources, arrived], axis=0)

    tiles2a = gathered(jnp.take(sources, order[:late_from], axis=0, mode="clip"))
    tiles2b = gathered(jnp.take(sources, order[late_from:held], axis=0, mode="clip"))
    misplaced = jnp.stack([jnp.max(fronts) - late_from, jnp.max(lengths) - held, jnp.max(lengths)])
    misplaced = lax.pmax(misplaced, "ffn")

    rows_f = tokens.astype(jnp.float32)
    center = jnp.mean(rows_f, axis=1, keepdims=True)
    spread = jnp.mean((rows_f - center) ** 2, axis=1, keepdims=True)
    normed = ((rows_f - center) / jnp.sqrt(spread + 1e-05) * ln_gain + ln_bias).astype(jnp.bfloat16)
    normed_blocks = normed.reshape(token_rows, second_blocks, side).transpose(1, 0, 2)
    normed_blocks = jnp.pad(normed_blocks, ((0, 1), (0, 0), (0, 0)))
    normed_blocks, misplaced = lax.optimization_barrier((normed_blocks, misplaced))
    some_late = jnp.max(misplaced[:2]) > 0

    (total,) = tile_pass(
        first_kernel,
        index1[:, :opening] // first_blocks,
        index1[:, :opening] % first_blocks,
        slot_ids[:opening] < count1[:, None],
        ffn,
        normed_blocks,
        tiles1,
        [fc1_bias.reshape(first_blocks, 1, side)],
        [fixed((first_blocks, 1, side))],
        [jax.ShapeDtypeStruct((first_blocks, token_rows, side), jnp.float32)],
        first_blocks,
        scratch=False,
    )
    (hidden,) = tile_pass(
        hidden_kernel,
        index1[:, opening:] // first_blocks,
        index1[:, opening:] % first_blocks,
        slot_ids[opening:] < count1[:, None],
        ffn,
        normed_blocks,
        tiles2a,
        [total],
        [fixed(total.shape)],
        [jax.ShapeDtypeStruct((first_blocks + 1, token_rows, side), jnp.bfloat16)],
        first_blocks,
    )

    def second_pass(places, live, tiles, steps=2, group=4):
        return tile_pass(
            partial_kernel,
            places // second_blocks,
            places % second_blocks,
            live,
            ffn,
            hidden,
            tiles,
            [],
            [],
            [
                jax.ShapeDtypeStruct((second_blocks, token_rows, side), jnp.float32),
                jax.ShapeDtypeStruct((token_rows, width), jnp.bfloat16),
            ],
            second_blocks,
            steps=steps,
            group=group,
            scratch=False,
        )

    def own_cols(value):
        return lax.dynamic_slice_in_dim(value, ffn * share, share, 1).astype(jnp.float32)

    def from_others(partial_value):
        branch = jnp.zeros((token_rows, share), jnp.float32)
        for shift in range(1, ffn_size):
            to = lax.rem(ffn + shift, ffn_size)
            arrived = lax.ppermute(
                lax.dynamic_slice_in_dim(partial_value, to * share, share, 1),
                "ffn",
                [(i, (i + shift) % ffn_size) for i in range(ffn_size)],
            )
            branch = branch + arrived.astype(jnp.float32)
        return branch

    in_front = total_ids < fronts[:, None]
    in_second = (total_ids >= left1[:, None]) & (total_ids < lengths[:, None])
    total, partial_value = second_pass(codes[:, :late_from], in_second[:, :late_from], tiles2a)
    last_codes = codes[:, late_from:held]
    last_own = (in_second & ~in_front)[:, late_from:held]
    branch = from_others(partial_value)

    def with_late(branch):
        chunk = slots // 4
        start = jnp.where(misplaced[0] > 0, late_from, held)
        late = in_second & (in_front | (total_ids >= held))

        def one_more(number, branch):
            at = start + number * chunk
            here = jnp.take(sources, lax.dynamic_slice_in_dim(order, at, chunk), axis=0, mode="clip")
            part = [lax.dynamic_slice_in_dim(v, at, chunk, 1) for v in (codes, late)]
            _, extra = second_pass(*part, gathered(here), steps=1, group=1)
            return branch + from_others(extra) + own_cols(extra)

        return lax.fori_loop(0, (misplaced[2] - start + chunk - 1) // chunk, one_more, branch)

    if not aligned:
        branch = lax.cond(some_late, with_late, lambda branch: branch, branch)
        more, _ = second_pass(last_codes, last_own, tiles2b)
        own = (total + more).transpose(1, 0, 2).reshape(token_rows, width)
        return (own_cols(tokens) + own_cols(own) + branch + fc2_bias).astype(jnp.bfloat16)

    share_blocks = share // side
    last_rows, last_cols = last_codes // second_blocks, last_codes % second_blocks % share_blocks
    last_plan = planned(last_rows, last_cols, last_own, share_blocks, first_blocks, 2, 4)
    bias_row = fc2_bias.reshape(1, share)
    last_plan, branch, bias_row = lax.optimization_barrier((last_plan, branch, bias_row))
    last_pass = functools.partial(
        tile_pass,
        result_kernel,
        last_rows,
        last_cols,
        last_own,
        ffn,
        hidden,
        tiles2b,
        more_specs=[
            pl.BlockSpec(
                (share_blocks, token_rows, side),
                lambda i, fields, counts, at: (at[0], 0, 0),
                pipeline_mode=pl.Buffered(1),
            ),
            pl.BlockSpec(
                (token_rows, share),
                lambda i, fields, counts, at: (0, at[0]),
                pipeline_mode=pl.Buffered(1),
            ),
            fixed((token_rows, share)),
            fixed((1, share)),
        ],
        out_shapes=[jax.ShapeDtypeStruct((token_rows, share), jnp.bfloat16)],
        blocks=share_blocks,
        steps=2,
        group=4,
        vmem=LAST_VMEM_BYTES,
        plan=last_plan,
    )

    def finished(branch):
        return last_pass(more=[total, tokens, branch, bias_row])[0]

    return lax.cond(some_late, lambda branch: finished(with_late(branch)), finished, branch)


def solution(mesh):
    placed = (
        P("blk", None),
        P(),
        P(),
        P("blk", "ffn", None, None, None),
        P("blk", "ffn", None),
        P("blk", "ffn"),
        P("ffn"),
        P("blk", "ffn", None, None, None),
        P("blk", "ffn", None),
        P("blk", "ffn"),
        P("ffn"),
    )
    return jax.shard_map(
        functools.partial(on_device, ffn_size=mesh.shape["ffn"]),
        mesh=mesh,
        in_specs=placed,
        out_specs=P("blk", "ffn"),
        check_vma=False,
    )
```

profile of v0, /device:TPU:0, one launch (start us, length us, event | category | flops | bytes accessed | tf_op | source)
XLA Modules:
  0.0 510.3 jit_solution(7957262794035051460)
XLA Ops:
  6.5 3.6 slice.121
  11.6 23.1 %all-gather.4 = s32[16,1,204]{2,1,0:T(1,128)S(1)} all-gather(s32[1,1,204]{2,1,0:T(1,128)S(1)} %add_bitcast_fusion), channel_id=1, replica_groups=mesh['blk'=16,'ffn'=2] {'blk'}, dimensions={0}, use_global_device_ids=true | all-gather | bytes 13872 | tf_op jit(solution)/shard_map/all_gather | solution.py:399
  37.0 36.9 %shard_map.111 = (s32[4560]{0:T(1024)}, s32[16]{0:T(128)}, s32[16]{0:T(128)}, s32[285]{0:T(512)S(1)}, s32[55]{0:T(128)}) custom-call(s32[1616]{0:T(1024)} %reshape.137.index_ref, s32[1616]{0:T(1024)} %reshape.151.own_ref, s32[16]{0:T(128)} %get-tuple-element.285.count_ref, s32[16]{0:T(128)} %get-tuple-element.284.left_ref, s32[1]{0:T(128)} %bitcast.11.at_ref), custom_call_target="tpu_custom_call" | custom-call | bytes 25856 | tf_op jit(solution)/shard_map/pallas_call | solution.py:350
  79.2 4.1 gather_fusion.1
  83.7 3.2 constant_dynamic-update-slice_fusion.4
  87.8 4.1 pad_maximum_fusion.1
  91.9 4.1 gather_fusion.2
  96.0 4.5 constant_dynamic-update-slice_fusion.3
  100.4 15.9 %collective-permute-done.2 = bf16[12,128,128]{2,1,0:T(8,128)(2,1)S(1)} collective-permute-done((bf16[12,128,128]{2,1,0:T(8,128)(2,1)}, bf16[12,128,128]{2,1,0:T(8,128)(2,1)S(1)}, u32[]{:S(2)}, u32[]{:S(2)}) %collective-permute-start.2) | collective-permute-done | bytes 393248 | tf_op jit(solution)/shard_map/ppermute | solution.py:418
  117.1 4.9 pad_maximum_fusion
  122.0 3.2 gather_fusion.3
  125.3 3.0 constant_dynamic-update-slice_fusion.2
  130.5 10.5 %collective-permute-done.3 = bf16[9,128,128]{2,1,0:T(8,128)(2,1)S(1)} collective-permute-done((bf16[9,128,128]{2,1,0:T(8,128)(2,1)S(1)}, bf16[9,128,128]{2,1,0:T(8,128)(2,1)S(1)}, u32[]{:S(2)}, u32[]{:S(2)}) %collective-permute-start.3) | collective-permute-done | bytes 294944 | tf_op jit(solution)/shard_map/ppermute | solution.py:418
  141.9 3.4 gather_fusion.4
  145.4 15.6 %collective-permute-done.4 = bf16[6,128,128]{2,1,0:T(8,128)(2,1)S(1)} collective-permute-done((bf16[6,128,128]{2,1,0:T(8,128)(2,1)S(1)}, bf16[6,128,128]{2,1,0:T(8,128)(2,1)S(1)}, u32[]{:S(2)}, u32[]{:S(2)}) %collective-permute-start.4) | collective-permute-done | bytes 196640 | tf_op jit(solution)/shard_map/ppermute | solution.py:418
  161.7 5.1 %gather_fusion.5 = bf16[69,128,128]{2,1,0:T(8,128)(2,1)} fusion(bf16[185,128,128]{2,1,0:T(8,128)(2,1)} %constant_dynamic-update-slice_fusion.5, s32[1024]{0:T(1024)S(1)} %pad_clamp_fusion.2), kind=kCustom, calls=%fused_computation.5 | custom fusion | bytes 4522260 | tf_op jit(solution)/shard_map/jit(_take)/gather | solution.py:425
  167.0 4.6 gather_fusion.6
  174.9 4.8 pmax.7
  188.1 3.5 fusion.7
  191.6 3.0 copy.19
  197.0 15.7 %shard_map.114 = (s32[1920]{0:T(1024)}, s32[4]{0:T(128)}) custom-call(s32[464]{0:T(512)} %reshape_reshape.14.row_ref, s32[464]{0:T(512)} %compare_select_fusion.1.col_ref), custom_call_target="tpu_custom_call" | custom-call | bytes 7424 | tf_op jit(solution)/shard_map/pallas_call | solution.py:61
  213.4 32.4 %shard_map.115 = (s32[3600]{0:T(1024)}, s32[4]{0:T(128)}) custom-call(s32[1152]{0:T(1024)} %reshape_reshape.15.row_ref, s32[1152]{0:T(1024)} %compare_select_fusion.col_ref), custom_call_target="tpu_custom_call" | custom-call | bytes 18432 | tf_op jit(solution)/shard_map/pallas_call | solution.py:61
  245.7 27.5 %shard_map.113 = (s32[3024]{0:T(1024)}, s32[2]{0:T(128)}) custom-call(s32[1104]{0:T(1024)} %reshape_reshape.13.row_ref, s32[1104]{0:T(1024)} %select_n.161.col_ref), custom_call_target="tpu_custom_call" | custom-call | bytes 17664 | tf_op jit(solution)/shard_map/pallas_call | solution.py:61
  273.3 57.0 %shard_map.116.sum_ref = f32[72,256,128]{2,1,0:T(8,128)} custom-call(s32[3600]{0:T(1024)} %get-tuple-element.274.field_ref, s32[4]{0:T(128)} %get-tuple-element.275.count_ref, s32[1]{0:T(128)} %bitcast.15.at_ref, bf16[37,256,128]{2,1,0:T(8,128)(2,1)} %pad.4.x_ref, bf16[16,72,128,128]{3,2,1,0:T(8,128)(2,1)} %bitcast.59, f32[72,1,128]{2,1,0:T(1,128)} %bitcast.63), custom_call_target="tpu_custom_call" | custom-call | flops 19327352832 | bytes 37748736 | tf_op jit(solution)/shard_map/pallas_call | solution.py:211
  330.3 63.2 %all-gather.12.cloned.1.call-done = bf16[1104,128,128]{2,1,0:T(8,128)(2,1)} async-done(((bf16[69,128,128]{2,1,0:T(8,128)(2,1)}), bf16[1104,128,128]{2,1,0:T(8,128)(2,1)}) %all-gather.12.cloned.1.call-update) | async-done | bytes 36175888 | tf_op jit(solution)/shard_map/all_gather | solution.py:395
  393.5 17.8 %shard_map.117.x_ref = bf16[73,256,128]{2,1,0:T(8,128)(2,1)S(1)} custom-call(s32[1920]{0:T(1024)} %get-tuple-element.269.field_ref, s32[4]{0:T(128)} %get-tuple-element.270.count_ref, s32[1]{0:T(128)} %bitcast.15.at_ref, bf16[37,256,128]{2,1,0:T(8,128)(2,1)} %pad.4.x_ref, bf16[16,69,128,128]{3,2,1,0:T(8,128)(2,1)} %bitcast.43, ...), custom_call_target="tpu_custom_call" | custom-call | flops 7784628224 | bytes 15204352 | tf_op jit(solution)/shard_map/pallas_call | solution.py:211
  411.3 41.1 %shard_map.118 = (f32[36,256,128]{2,1,0:T(8,128)}, bf16[256,4608]{1,0:T(8,128)(2,1)}) custom-call(s32[3024]{0:T(1024)} %get-tuple-element.267.field_ref, s32[2]{0:T(128)} %get-tuple-element.268.count_ref, s32[1]{0:T(128)} %bitcast.15.at_ref, bf16[73,256,128]{2,1,0:T(8,128)(2,1)S(1)} %shard_map.117.x_ref, bf16[16,69,128,128]{3,2,1,0:T(8,128)(2,1)} %bitcast.44), custom_call_target="tpu_custom_call" | custom-call | flops 18522046464 | bytes 36175872 | tf_op jit(solution)/shard_map/pallas_call | solution.py:211
  458.5 13.8 %shard_map.112 = (s32[1440]{0:T(1024)}, s32[2]{0:T(128)}) custom-call(s32[528]{0:T(1024)} %reshape_reshape.12.row_ref, s32[528]{0:T(1024)} %select_n.157.col_ref), custom_call_target="tpu_custom_call" | custom-call | bytes 8448 | tf_op jit(solution)/shard_map/pallas_call | solution.py:61
  472.3 9.9 %collective-permute-done.5 = bf16[256,2304]{1,0:T(8,128)(2,1)S(1)} collective-permute-done((bf16[256,2304]{1,0:T(8,128)(2,1)S(1)}, bf16[256,2304]{1,0:T(8,128)(2,1)S(1)}, u32[]{:S(2)}, u32[]{:S(2)}) %collective-permute-start.5) | collective-permute-done | bytes 1179680 | tf_op jit(solution)/shard_map/ppermute | solution.py:495
  482.4 4.3 all-gather.16.cloned.1.call-done
  486.7 16.0 %conditional.1 = (bf16[256,2304]{1,0:T(8,128)(2,1)S(1)}) conditional(s32[]{:T(128)} %convert_element_type.29, (s32[]{:T(128)}, s32[1440]{0:T(1024)}, s32[2]{0:T(128)}, bf16[73,256,128]{2,1,0:T(8,128)(2,1)}, bf16[16,33,128,128]{3,2,1,0:T(8,128)(2,1)}, /*index=5*/f32[36,256,128]{2,1,0:T(8,128)}, bf16[256,4608]{1,0:T(8,128)(2,1)}, ...), branch_computations={%region_6.7_spmd, %region_7.10_spmd} | conditional | flops 15571631104 | bytes 88062056 | solution.py:569
  486.7 16.0 %branch_0_fun.1 = bf16[256,2304]{1,0:T(8,128)(2,1)S(1)} custom-call(s32[1440]{0:T(1024)} %get-tuple-element.197.field_ref, s32[2]{0:T(128)} %get-tuple-element.198.count_ref, s32[1]{0:T(128)} %bitcast.at_ref, bf16[73,256,128]{2,1,0:T(8,128)(2,1)} %get-tuple-element.200.x_ref, bf16[16,33,128,128]{3,2,1,0:T(8,128)(2,1)} %get-tuple-element.201.w_ref, ...), custom_call_target="tpu_custom_call" | custom-call | flops 8858370048 | bytes 17301504 | tf_op jit(solution)/shard_map/cond/branch_0_fun/pallas_call | solution.py:211
  (130 shorter events, 33.8 us)
Async XLA Ops:
  6.5 4.9 copy-start.19
  6.5 5.0 copy-start.20
  6.5 70.3 %copy-start = (bf16[1,1,101,128,128]{4,3,2,1,0:T(8,128)(2,1)S(1)}, bf16[1,1,101,128,128]{4,3,2,1,0:T(8,128)(2,1)}, u32[]{:S(2)}) copy-start(bf16[1,1,101,128,128]{4,3,2,1,0:T(8,128)(2,1)} %param.22) | copy-start | bytes 9928708
  6.5 266.7 %all-gather.14.cloned.1.call-start = ((), (), s32[]{:S(2)}) async-start(), calls=%async_computation.1 | async-start | bytes 40108032 | tf_op jit(solution)/shard_map/all_gather | solution.py:395
  10.1 383.3 %all-gather.12.cloned.1.call-start = ((), (), s32[]{:S(2)}) async-start(), calls=%async_computation | async-start | bytes 38436864 | tf_op jit(solution)/shard_map/all_gather | solution.py:395
  73.9 93.0 %copy-start.22 = (s32[285]{0:T(512)}, s32[285]{0:T(512)S(1)}, u32[]{:S(2)}) copy-start(s32[285]{0:T(512)S(1)} %get-tuple-element.273) | copy-start | bytes 3424
  75.9 0.9 copy-start.1
  76.8 6.6 %copy-start.18 = (s32[55]{0:T(128)S(1)}, s32[55]{0:T(128)}, u32[]{:S(2)}) copy-start(s32[55]{0:T(128)} %get-tuple-element.272) | copy-start | bytes 664
  83.3 3.6 collective-permute-start.1
  86.9 0.9 copy-start.3
  96.0 20.3 %collective-permute-start.2 = (bf16[12,128,128]{2,1,0:T(8,128)(2,1)}, bf16[12,128,128]{2,1,0:T(8,128)(2,1)S(1)}, u32[]{:S(2)}, u32[]{:S(2)}) collective-permute-start(bf16[12,128,128]{2,1,0:T(8,128)(2,1)} %gather_fusion.2), channel_id=1, source_target_pairs={{0,4},{2,6},{4,0},{6,2},{8,12},{10,14},{12,8},{14,10},{16,20},{18,... | collective-permute-start | bytes 1179656 | tf_op jit(solution)/shard_map/ppermute | solution.py:418
  96.0 21.1 %copy-start.2 = (bf16[29,128,128]{2,1,0:T(8,128)(2,1)S(1)}, bf16[29,128,128]{2,1,0:T(8,128)(2,1)}, u32[]{:S(2)}) copy-start(bf16[29,128,128]{2,1,0:T(8,128)(2,1)} %copy-done.1) | copy-start | bytes 2850820
  96.0 21.1 %copy-start.4 = (bf16[28,128,128]{2,1,0:T(8,128)(2,1)S(1)}, bf16[28,128,128]{2,1,0:T(8,128)(2,1)}, u32[]{:S(2)}) copy-start(bf16[28,128,128]{2,1,0:T(8,128)(2,1)} %copy-done.3) | copy-start | bytes 2752516
  116.3 0.7 copy-start.6
  125.2 15.7 %collective-permute-start.3 = (bf16[9,128,128]{2,1,0:T(8,128)(2,1)S(1)}, bf16[9,128,128]{2,1,0:T(8,128)(2,1)S(1)}, u32[]{:S(2)}, u32[]{:S(2)}) collective-permute-start(bf16[9,128,128]{2,1,0:T(8,128)(2,1)S(1)} %gather_fusion.3), channel_id=1, source_target_pairs={{0,8},{2,10},{4,12},{6,14},{8,0},{10,2},{12,4},{14,6},{16,24},{18,... | collective-permute-start | bytes 884744 | tf_op jit(solution)/shard_map/ppermute | solution.py:418
  145.3 15.7 %collective-permute-start.4 = (bf16[6,128,128]{2,1,0:T(8,128)(2,1)S(1)}, bf16[6,128,128]{2,1,0:T(8,128)(2,1)S(1)}, u32[]{:S(2)}, u32[]{:S(2)}) collective-permute-start(bf16[6,128,128]{2,1,0:T(8,128)(2,1)S(1)} %gather_fusion.4), channel_id=1, source_target_pairs={{0,16},{2,18},{4,20},{6,22},{8,24},{10,26},{12,28},{14,30},{16,0},... | collective-permute-start | bytes 589832 | tf_op jit(solution)/shard_map/ppermute | solution.py:418
  161.7 9.9 %copy-start.17 = (s32[16]{0:T(128)S(1)}, s32[16]{0:T(128)}, u32[]{:S(2)}) copy-start(s32[16]{0:T(128)} %get-tuple-element.262) | copy-start | bytes 196
  161.7 10.6 %copy-start.16 = (s32[16]{0:T(128)S(1)}, s32[16]{0:T(128)}, u32[]{:S(2)}) copy-start(s32[16]{0:T(128)} %get-tuple-element.261) | copy-start | bytes 196
  161.7 18.9 %copy-start.10 = (s32[4560]{0:T(1024)S(1)}, s32[4560]{0:T(1024)}, u32[]{:S(2)}) copy-start(s32[4560]{0:T(1024)} %get-tuple-element.264) | copy-start | bytes 54724
  161.7 20.7 %copy-start.14 = (s32[16]{0:T(128)S(1)}, s32[16]{0:T(128)}, u32[]{:S(2)}) copy-start(s32[16]{0:T(128)} %get-tuple-element.284.left_ref) | copy-start | bytes 196
  166.9 319.7 %all-gather.16.cloned.1.call-start = ((), (), s32[]{:S(2)}) async-start(), calls=%async_computation.2 | async-start | bytes 18382848 | tf_op jit(solution)/shard_map/all_gather | solution.py:395
  180.7 2.6 copy-start.7
  183.9 4.2 copy-start.11
  183.9 4.2 copy-start.12
  411.3 41.2 %copy-start.5 = (bf16[73,256,128]{2,1,0:T(8,128)(2,1)}, bf16[73,256,128]{2,1,0:T(8,128)(2,1)S(1)}, u32[]{:S(2)}) copy-start(bf16[73,256,128]{2,1,0:T(8,128)(2,1)S(1)} %shard_map.117.x_ref) | copy-start | bytes 14352388
  411.3 44.0 %copy-start.13 = (f32[2304]{0:T(1024)S(1)}, f32[2304]{0:T(1024)}, u32[]{:S(2)}) copy-start(f32[2304]{0:T(1024)} %param.25) | copy-start | bytes 27652
  411.3 44.6 %copy-start.8 = (s32[16,285]{1,0:T(8,128)S(1)}, s32[16,285]{1,0:T(8,128)}, u32[]{:S(2)}) copy-start(s32[16,285]{1,0:T(8,128)} %copy-done.7) | copy-start | bytes 54724
  411.3 46.1 %copy-start.15 = (s32[3]{0:T(128)S(1)}, s32[3]{0:T(128)}, u32[]{:S(2)}) copy-start(s32[3]{0:T(128)} %pmax.7) | copy-start | bytes 40
  453.8 28.5 %collective-permute-start.5 = (bf16[256,2304]{1,0:T(8,128)(2,1)S(1)}, bf16[256,2304]{1,0:T(8,128)(2,1)S(1)}, u32[]{:S(2)}, u32[]{:S(2)}) collective-permute-start(bf16[256,2304]{1,0:T(8,128)(2,1)S(1)} %constant_dynamic-slice_fusion.1), channel_id=1, source_target_pairs={{0,1},{1,0},{2,3},{3,2},{4,5},{5,4},{6,7},{7,6},{8,9},{9,8},{10,11... | collective-permute-start | bytes 3538952 | tf_op jit(solution)/shard_map/ppermute | solution.py:495
  502.7 1.0 copy-start.23
Sparse Core Ops, SparseCore 0:
  10.2 201.1 all-gather.13
  213.0 180.3 all-gather.11
  395.1 91.5 all-gather.15
where the time goes:
time: 514 us; the launch traced here: 510 us
  Pallas kernels  258 us (50%)
  waiting for transfers between devices  119 us (23%)
  local copies, waits for them, and re-layouts  63.9 us (12%)
  blocking collectives  27.9 us (5%)
  other arithmetic  22.3 us (4%)
  between operations  16.6 us (3%)
    pallas_call x4, Pallas kernels, tile_pass(): pl.pallas_call(functools.partial(kernel, group), out_shape=out_shapes, gr...  132 us
    pallas_call x4, Pallas kernels, group_up(): pl.pallas_call(functools.partial(group_kernel, group, size, zero_row), ou...  89.4 us
    all_gather x3, waiting for transfers between devices, gathered(): lax.all_gather(value, 'blk', axis=0, tiled=True)  67.5 us
    ppermute x4, waiting for transfers between devices, on_device(): lax.ppermute(jnp.take(sources, sending, axis=0, mode='clip'), 'blk', [(i,...  42 us
    pallas_call x1, Pallas kernels, laid_out(): pl.pallas_call(functools.partial(layout_kernel, levels, capacity), out_sh...  36.9 us
    all_gather x1, blocking collectives, on_device(): meta = lax.all_gather(meta, 'blk', axis=0, tiled=True)  23.1 us
    unnamed x50, local copies, waits for them, and re-layouts  19.3 us
    gather x4, local copies, waits for them, and re-layouts, on_device(): jnp.take(sources, sending, axis=0, mode='clip')  14.7 us
  transfers between devices with their start and end apart: 8, of which 6 were waited for; matrix products, arithmetic and copies ran while one was open for 15% of the time, Pallas kernels for 47%

commit v1 on v0

--- a/solution.py
+++ b/solution.py
@@ -7,9 +7,9 @@
 from jax.experimental.pallas import tpu as pltpu
 from jax.sharding import PartitionSpec as P
 
-UNROLL = 4
+UNROLL = 8
 VMEM_BYTES = 56 * 1024 * 1024
-LAST_VMEM_BYTES = 36 * 1024 * 1024
+LAST_VMEM_BYTES = 26 * 1024 * 1024
 
 
 def group_kernel(group, size, zero_row, row_ref, col_ref, field_ref, count_ref, fill_ref, open_ref):
@@ -529,7 +529,7 @@
 
     share_blocks = share // side
     last_rows, last_cols = last_codes // second_blocks, last_codes % second_blocks % share_blocks
-    last_plan = planned(last_rows, last_cols, last_own, share_blocks, first_blocks, 2, 4)
+    last_plan = planned(last_rows, last_cols, last_own, share_blocks, first_blocks, 4, 4)
     bias_row = fc2_bias.reshape(1, share)
     last_plan, branch, bias_row = lax.optimization_barrier((last_plan, branch, bias_row))
     last_pass = functools.partial(
@@ -557,7 +557,7 @@
         ],
         out_shapes=[jax.ShapeDtypeStruct((token_rows, share), jnp.bfloat16)],
         blocks=share_blocks,
-        steps=2,
+        steps=4,
         group=4,
         vmem=LAST_VMEM_BYTES,
         plan=last_plan,

time: 514 us -> 513 us (level)
  waiting for transfers between devices: 119 us -> 135 us
  Pallas kernels: 258 us -> 243 us
    all_gather x3, waiting for transfers between devices: 67.5 us -> 84.3 us  [gathered(): lax.all_gather(value, 'blk', axis=0, tiled=True)]
    pallas_call x4, Pallas kernels: 132 us -> 116 us  [tile_pass(): pl.pallas_call(functools.partial(kernel, group), out_shape=out_shapes, gr...]
  transfers between devices with their start and end apart: 8 -> 8, of which waited for: 6 -> 6; matrix products, arithmetic and copies ran while one was open for 15% -> 15% of each run, Pallas kernels for 47% -> 44%
where the time goes in v1:
time: 513 us; the launch traced here: 512 us
  Pallas kernels  243 us (47%)
  waiting for transfers between devices  135 us (26%)
  local copies, waits for them, and re-layouts  64 us (12%)
  blocking collectives  28.4 us (6%)
  other arithmetic  22.3 us (4%)
  between operations  16.6 us (3%)
    pallas_call x4, Pallas kernels, tile_pass(): pl.pallas_call(functools.partial(kernel, group), out_shape=out_shapes, gr...  116 us
    pallas_call x4, Pallas kernels, group_up(): pl.pallas_call(functools.partial(group_kernel, group, size, zero_row), ou...  90.2 us
    all_gather x3, waiting for transfers between devices, gathered(): lax.all_gather(value, 'blk', axis=0, tiled=True)  84.3 us
    ppermute x4, waiting for transfers between devices, on_device(): lax.ppermute(jnp.take(sources, sending, axis=0, mode='clip'), 'blk', [(i,...  41.9 us
    pallas_call x1, Pallas kernels, laid_out(): pl.pallas_call(functools.partial(layout_kernel, levels, capacity), out_sh...  37.2 us
    all_gather x1, blocking collectives, on_device(): meta = lax.all_gather(meta, 'blk', axis=0, tiled=True)  23.1 us
    unnamed x50, local copies, waits for them, and re-layouts  19.6 us
    gather x4, local copies, waits for them, and re-layouts, on_device(): jnp.take(sources, sending, axis=0, mode='clip')  14.5 us
  transfers between devices with their start and end apart: 8, of which 6 were waited for; matrix products, arithmetic and copies ran while one was open for 15% of the time, Pallas kernels for 44%

profile of v1, /device:TPU:0, one launch (start us, length us, event | category | flops | bytes accessed | tf_op | source)
XLA Modules:
  0.0 511.9 jit_solution(10337317415947490294)
XLA Ops:
  6.5 3.6 slice.121
  11.6 23.1 %all-gather.4 = s32[16,1,204]{2,1,0:T(1,128)S(1)} all-gather(s32[1,1,204]{2,1,0:T(1,128)S(1)} %add_bitcast_fusion), channel_id=1, replica_groups=mesh['blk'=16,'ffn'=2] {'blk'}, dimensions={0}, use_global_device_ids=true | all-gather | bytes 13872 | tf_op jit(solution)/shard_map/all_gather | solution.py:399
  37.0 37.2 %shard_map.111 = (s32[4560]{0:T(1024)}, s32[16]{0:T(128)}, s32[16]{0:T(128)}, s32[285]{0:T(512)S(1)}, s32[55]{0:T(128)}) custom-call(s32[1616]{0:T(1024)} %reshape.137.index_ref, s32[1616]{0:T(1024)} %reshape.151.own_ref, s32[16]{0:T(128)} %get-tuple-element.285.count_ref, s32[16]{0:T(128)} %get-tuple-element.284.left_ref, s32[1]{0:T(128)} %bitcast.11.at_ref), custom_call_target="tpu_custom_call" | custom-call | bytes 25856 | tf_op jit(solution)/shard_map/pallas_call | solution.py:350
  79.4 4.0 gather_fusion.1
  83.9 3.2 constant_dynamic-update-slice_fusion.4
  88.0 4.1 pad_maximum_fusion.1
  92.1 4.0 gather_fusion.2
  96.1 4.5 constant_dynamic-update-slice_fusion.3
  100.6 15.9 %collective-permute-done.2 = bf16[12,128,128]{2,1,0:T(8,128)(2,1)S(1)} collective-permute-done((bf16[12,128,128]{2,1,0:T(8,128)(2,1)}, bf16[12,128,128]{2,1,0:T(8,128)(2,1)S(1)}, u32[]{:S(2)}, u32[]{:S(2)}) %collective-permute-start.2) | collective-permute-done | bytes 393248 | tf_op jit(solution)/shard_map/ppermute | solution.py:418
  117.2 4.9 pad_maximum_fusion
  122.1 3.2 gather_fusion.3
  125.4 3.1 constant_dynamic-update-slice_fusion.2
  130.7 10.4 %collective-permute-done.3 = bf16[9,128,128]{2,1,0:T(8,128)(2,1)S(1)} collective-permute-done((bf16[9,128,128]{2,1,0:T(8,128)(2,1)S(1)}, bf16[9,128,128]{2,1,0:T(8,128)(2,1)S(1)}, u32[]{:S(2)}, u32[]{:S(2)}) %collective-permute-start.3) | collective-permute-done | bytes 294944 | tf_op jit(solution)/shard_map/ppermute | solution.py:418
  142.0 3.4 gather_fusion.4
  145.5 15.6 %collective-permute-done.4 = bf16[6,128,128]{2,1,0:T(8,128)(2,1)S(1)} collective-permute-done((bf16[6,128,128]{2,1,0:T(8,128)(2,1)S(1)}, bf16[6,128,128]{2,1,0:T(8,128)(2,1)S(1)}, u32[]{:S(2)}, u32[]{:S(2)}) %collective-permute-start.4) | collective-permute-done | bytes 196640 | tf_op jit(solution)/shard_map/ppermute | solution.py:418
  161.8 5.1 %gather_fusion.5 = bf16[69,128,128]{2,1,0:T(8,128)(2,1)} fusion(bf16[185,128,128]{2,1,0:T(8,128)(2,1)} %constant_dynamic-update-slice_fusion.5, s32[1024]{0:T(1024)S(1)} %pad_clamp_fusion.2), kind=kCustom, calls=%fused_computation.5 | custom fusion | bytes 4522260 | tf_op jit(solution)/shard_map/jit(_take)/gather | solution.py:425
  167.2 4.6 gather_fusion.6
  175.0 5.3 %pmax.7 = s32[3]{0:T(128)} all-reduce(s32[3]{0:T(128)S(1)} %pad_add_fusion), channel_id=1, replica_groups=mesh['blk'=16,'ffn'=2] {'ffn'}, use_global_device_ids=true, to_apply=%region_4.5 | all-reduce | flops 3 | bytes 24 | tf_op jit(solution)/shard_map/pmax | solution.py:428
  189.0 3.5 fusion.7
  192.5 3.0 copy.19
  197.8 15.7 %shard_map.114 = (s32[1920]{0:T(1024)}, s32[4]{0:T(128)}) custom-call(s32[464]{0:T(512)} %reshape_reshape.14.row_ref, s32[464]{0:T(512)} %compare_select_fusion.1.col_ref), custom_call_target="tpu_custom_call" | custom-call | bytes 7424 | tf_op jit(solution)/shard_map/pallas_call | solution.py:61
  214.2 32.5 %shard_map.115 = (s32[3680]{0:T(1024)}, s32[4]{0:T(128)}) custom-call(s32[1152]{0:T(1024)} %reshape_reshape.15.row_ref, s32[1152]{0:T(1024)} %compare_select_fusion.col_ref), custom_call_target="tpu_custom_call" | custom-call | bytes 18432 | tf_op jit(solution)/shard_map/pallas_call | solution.py:61
  246.6 27.5 %shard_map.113 = (s32[3024]{0:T(1024)}, s32[2]{0:T(128)}) custom-call(s32[1104]{0:T(1024)} %reshape_reshape.13.row_ref, s32[1104]{0:T(1024)} %select_n.161.col_ref), custom_call_target="tpu_custom_call" | custom-call | bytes 17664 | tf_op jit(solution)/shard_map/pallas_call | solution.py:61
  274.2 46.0 %shard_map.116.sum_ref = f32[72,256,128]{2,1,0:T(8,128)} custom-call(s32[3680]{0:T(1024)} %get-tuple-element.274.field_ref, s32[4]{0:T(128)} %get-tuple-element.275.count_ref, s32[1]{0:T(128)} %bitcast.15.at_ref, bf16[37,256,128]{2,1,0:T(8,128)(2,1)} %pad.4.x_ref, bf16[16,72,128,128]{3,2,1,0:T(8,128)(2,1)} %bitcast.59, f32[72,1,128]{2,1,0:T(1,128)} %bitcast.63), custom_call_target="tpu_custom_call" | custom-call | flops 19327352832 | bytes 37748736 | tf_op jit(solution)/shard_map/pallas_call | solution.py:211
  320.2 73.3 %all-gather.12.cloned.1.call-done = bf16[1104,128,128]{2,1,0:T(8,128)(2,1)} async-done(((bf16[69,128,128]{2,1,0:T(8,128)(2,1)}), bf16[1104,128,128]{2,1,0:T(8,128)(2,1)}) %all-gather.12.cloned.1.call-update) | async-done | bytes 36175888 | tf_op jit(solution)/shard_map/all_gather | solution.py:395
  393.5 17.9 %shard_map.117.x_ref = bf16[73,256,128]{2,1,0:T(8,128)(2,1)S(1)} custom-call(s32[1920]{0:T(1024)} %get-tuple-element.269.field_ref, s32[4]{0:T(128)} %get-tuple-element.270.count_ref, s32[1]{0:T(128)} %bitcast.15.at_ref, bf16[37,256,128]{2,1,0:T(8,128)(2,1)} %pad.4.x_ref, bf16[16,69,128,128]{3,2,1,0:T(8,128)(2,1)} %bitcast.43, ...), custom_call_target="tpu_custom_call" | custom-call | flops 7784628224 | bytes 15204352 | tf_op jit(solution)/shard_map/pallas_call | solution.py:211
  411.4 34.4 %shard_map.118 = (f32[36,256,128]{2,1,0:T(8,128)}, bf16[256,4608]{1,0:T(8,128)(2,1)}) custom-call(s32[3024]{0:T(1024)} %get-tuple-element.267.field_ref, s32[2]{0:T(128)} %get-tuple-element.268.count_ref, s32[1]{0:T(128)} %bitcast.15.at_ref, bf16[73,256,128]{2,1,0:T(8,128)(2,1)S(1)} %shard_map.117.x_ref, bf16[16,69,128,128]{3,2,1,0:T(8,128)(2,1)} %bitcast.44), custom_call_target="tpu_custom_call" | custom-call | flops 18522046464 | bytes 36175872 | tf_op jit(solution)/shard_map/pallas_call | solution.py:211
  451.8 14.5 %shard_map.112 = (s32[1728]{0:T(1024)}, s32[4]{0:T(128)}) custom-call(s32[528]{0:T(1024)} %reshape_reshape.12.row_ref, s32[528]{0:T(1024)} %select_n.157.col_ref), custom_call_target="tpu_custom_call" | custom-call | bytes 8448 | tf_op jit(solution)/shard_map/pallas_call | solution.py:61
  466.3 9.2 %collective-permute-done.5 = bf16[256,2304]{1,0:T(8,128)(2,1)S(1)} collective-permute-done((bf16[256,2304]{1,0:T(8,128)(2,1)S(1)}, bf16[256,2304]{1,0:T(8,128)(2,1)S(1)}, u32[]{:S(2)}, u32[]{:S(2)}) %collective-permute-start.5) | collective-permute-done | bytes 1179680 | tf_op jit(solution)/shard_map/ppermute | solution.py:495
  475.6 11.0 %all-gather.16.cloned.1.call-done = bf16[528,128,128]{2,1,0:T(8,128)(2,1)} async-done(((bf16[33,128,128]{2,1,0:T(8,128)(2,1)}), bf16[528,128,128]{2,1,0:T(8,128)(2,1)}) %all-gather.16.cloned.1.call-update) | async-done | bytes 17301520 | tf_op jit(solution)/shard_map/all_gather | solution.py:395
  486.7 17.7 %conditional.1 = (bf16[256,2304]{1,0:T(8,128)(2,1)S(1)}) conditional(s32[]{:T(128)} %convert_element_type.29, (s32[]{:T(128)}, s32[1728]{0:T(1024)}, s32[4]{0:T(128)}, bf16[73,256,128]{2,1,0:T(8,128)(2,1)}, bf16[16,33,128,128]{3,2,1,0:T(8,128)(2,1)}, /*index=5*/f32[36,256,128]{2,1,0:T(8,128)}, bf16[256,4608]{1,0:T(8,128)(2,1)}, ...), branch_computations={%region_6.7_spmd, %region_7.10_spmd} | conditional | flops 15571631104 | bytes 88066664 | solution.py:569
  486.7 17.6 %branch_0_fun.1 = bf16[256,2304]{1,0:T(8,128)(2,1)S(1)} custom-call(s32[1728]{0:T(1024)} %get-tuple-element.197.field_ref, s32[4]{0:T(128)} %get-tuple-element.198.count_ref, s32[1]{0:T(128)} %bitcast.at_ref, bf16[73,256,128]{2,1,0:T(8,128)(2,1)} %get-tuple-element.200.x_ref, bf16[16,33,128,128]{3,2,1,0:T(8,128)(2,1)} %get-tuple-element.201.w_ref, ...), custom_call_target="tpu_custom_call" | custom-call | flops 8858370048 | bytes 17301504 | tf_op jit(solution)/shard_map/cond/branch_0_fun/pallas_call | solution.py:211
  (130 shorter events, 34.0 us)
Async XLA Ops:
  6.5 4.9 copy-start.19
  6.5 5.0 copy-start.20
  6.5 70.5 %copy-start = (bf16[1,1,101,128,128]{4,3,2,1,0:T(8,128)(2,1)S(1)}, bf16[1,1,101,128,128]{4,3,2,1,0:T(8,128)(2,1)}, u32[]{:S(2)}) copy-start(bf16[1,1,101,128,128]{4,3,2,1,0:T(8,128)(2,1)} %param.22) | copy-start | bytes 9928708
  6.5 267.7 %all-gather.14.cloned.1.call-start = ((), (), s32[]{:S(2)}) async-start(), calls=%async_computation.1 | async-start | bytes 40108032 | tf_op jit(solution)/shard_map/all_gather | solution.py:395
  10.1 383.3 %all-gather.12.cloned.1.call-start = ((), (), s32[]{:S(2)}) async-start(), calls=%async_computation | async-start | bytes 38436864 | tf_op jit(solution)/shard_map/all_gather | solution.py:395
  74.1 92.9 %copy-start.22 = (s32[285]{0:T(512)}, s32[285]{0:T(512)S(1)}, u32[]{:S(2)}) copy-start(s32[285]{0:T(512)S(1)} %get-tuple-element.273) | copy-start | bytes 3424
  76.1 0.9 copy-start.1
  77.1 6.6 %copy-start.18 = (s32[55]{0:T(128)S(1)}, s32[55]{0:T(128)}, u32[]{:S(2)}) copy-start(s32[55]{0:T(128)} %get-tuple-element.272) | copy-start | bytes 664
  83.4 3.7 collective-permute-start.1
  87.1 0.9 copy-start.3
  96.1 20.3 %collective-permute-start.2 = (bf16[12,128,128]{2,1,0:T(8,128)(2,1)}, bf16[12,128,128]{2,1,0:T(8,128)(2,1)S(1)}, u32[]{:S(2)}, u32[]{:S(2)}) collective-permute-start(bf16[12,128,128]{2,1,0:T(8,128)(2,1)} %gather_fusion.2), channel_id=1, source_target_pairs={{0,4},{2,6},{4,0},{6,2},{8,12},{10,14},{12,8},{14,10},{16,20},{18,... | collective-permute-start | bytes 1179656 | tf_op jit(solution)/shard_map/ppermute | solution.py:418
  96.1 21.1 %copy-start.2 = (bf16[29,128,128]{2,1,0:T(8,128)(2,1)S(1)}, bf16[29,128,128]{2,1,0:T(8,128)(2,1)}, u32[]{:S(2)}) copy-start(bf16[29,128,128]{2,1,0:T(8,128)(2,1)} %copy-done.1) | copy-start | bytes 2850820
  96.1 21.1 %copy-start.4 = (bf16[28,128,128]{2,1,0:T(8,128)(2,1)S(1)}, bf16[28,128,128]{2,1,0:T(8,128)(2,1)}, u32[]{:S(2)}) copy-start(bf16[28,128,128]{2,1,0:T(8,128)(2,1)} %copy-done.3) | copy-start | bytes 2752516
  116.4 0.7 copy-start.6
  125.3 15.7 %collective-permute-start.3 = (bf16[9,128,128]{2,1,0:T(8,128)(2,1)S(1)}, bf16[9,128,128]{2,1,0:T(8,128)(2,1)S(1)}, u32[]{:S(2)}, u32[]{:S(2)}) collective-permute-start(bf16[9,128,128]{2,1,0:T(8,128)(2,1)S(1)} %gather_fusion.3), channel_id=1, source_target_pairs={{0,8},{2,10},{4,12},{6,14},{8,0},{10,2},{12,4},{14,6},{16,24},{18,... | collective-permute-start | bytes 884744 | tf_op jit(solution)/shard_map/ppermute | solution.py:418
  145.4 15.8 %collective-permute-start.4 = (bf16[6,128,128]{2,1,0:T(8,128)(2,1)S(1)}, bf16[6,128,128]{2,1,0:T(8,128)(2,1)S(1)}, u32[]{:S(2)}, u32[]{:S(2)}) collective-permute-start(bf16[6,128,128]{2,1,0:T(8,128)(2,1)S(1)} %gather_fusion.4), channel_id=1, source_target_pairs={{0,16},{2,18},{4,20},{6,22},{8,24},{10,26},{12,28},{14,30},{16,0},... | collective-permute-start | bytes 589832 | tf_op jit(solution)/shard_map/ppermute | solution.py:418
  161.8 9.9 %copy-start.17 = (s32[16]{0:T(128)S(1)}, s32[16]{0:T(128)}, u32[]{:S(2)}) copy-start(s32[16]{0:T(128)} %get-tuple-element.262) | copy-start | bytes 196
  161.8 10.6 %copy-start.16 = (s32[16]{0:T(128)S(1)}, s32[16]{0:T(128)}, u32[]{:S(2)}) copy-start(s32[16]{0:T(128)} %get-tuple-element.261) | copy-start | bytes 196
  161.8 19.4 %copy-start.10 = (s32[4560]{0:T(1024)S(1)}, s32[4560]{0:T(1024)}, u32[]{:S(2)}) copy-start(s32[4560]{0:T(1024)} %get-tuple-element.264) | copy-start | bytes 54724
  161.8 21.3 %copy-start.14 = (s32[16]{0:T(128)S(1)}, s32[16]{0:T(128)}, u32[]{:S(2)}) copy-start(s32[16]{0:T(128)} %get-tuple-element.284.left_ref) | copy-start | bytes 196
  167.0 319.6 %all-gather.16.cloned.1.call-start = ((), (), s32[]{:S(2)}) async-start(), calls=%async_computation.2 | async-start | bytes 18382848 | tf_op jit(solution)/shard_map/all_gather | solution.py:395
  181.3 2.6 copy-start.7
  184.6 4.4 copy-start.11
  184.6 4.4 copy-start.12
  411.3 34.5 %copy-start.5 = (bf16[73,256,128]{2,1,0:T(8,128)(2,1)}, bf16[73,256,128]{2,1,0:T(8,128)(2,1)S(1)}, u32[]{:S(2)}) copy-start(bf16[73,256,128]{2,1,0:T(8,128)(2,1)S(1)} %shard_map.117.x_ref) | copy-start | bytes 14352388
  411.4 37.2 %copy-start.13 = (f32[2304]{0:T(1024)S(1)}, f32[2304]{0:T(1024)}, u32[]{:S(2)}) copy-start(f32[2304]{0:T(1024)} %param.25) | copy-start | bytes 27652
  411.4 37.7 %copy-start.8 = (s32[16,285]{1,0:T(8,128)S(1)}, s32[16,285]{1,0:T(8,128)}, u32[]{:S(2)}) copy-start(s32[16,285]{1,0:T(8,128)} %copy-done.7) | copy-start | bytes 54724
  411.4 39.3 %copy-start.15 = (s32[3]{0:T(128)S(1)}, s32[3]{0:T(128)}, u32[]{:S(2)}) copy-start(s32[3]{0:T(128)} %pmax.7) | copy-start | bytes 40
  447.2 28.3 %collective-permute-start.5 = (bf16[256,2304]{1,0:T(8,128)(2,1)S(1)}, bf16[256,2304]{1,0:T(8,128)(2,1)S(1)}, u32[]{:S(2)}, u32[]{:S(2)}) collective-permute-start(bf16[256,2304]{1,0:T(8,128)(2,1)S(1)} %constant_dynamic-slice_fusion.1), channel_id=1, source_target_pairs={{0,1},{1,0},{2,3},{3,2},{4,5},{5,4},{6,7},{7,6},{8,9},{9,8},{10,11... | collective-permute-start | bytes 3538952 | tf_op jit(solution)/shard_map/ppermute | solution.py:495
  504.3 1.0 copy-start.23
Sparse Core Ops, SparseCore 0:
  10.2 201.1 all-gather.13
  213.0 180.3 all-gather.11
  395.1 91.5 all-gather.15

commit v2 on v1

--- a/solution.py
+++ b/solution.py
@@ -236,8 +236,9 @@
 def layout_kernel(
     levels, capacity, index_ref, own_ref, count_ref, left_ref, at_ref,
     code_ref, front_count_ref, length_ref, order_ref, send_ref,
-    place_ref, source_ref, fronts, backs, sent_ref,
+    place_ref, source_ref, late_place_ref, late_source_ref, fronts, backs, kept_fronts, kept_backs, sent_ref,
 ):
+    late_room = late_place_ref.shape[0] // (2 * count_ref.shape[0])
     shards = count_ref.shape[0]
     slots = index_ref.shape[0] // shards
     total = order_ref.shape[0]
@@ -269,10 +270,15 @@
             return front + 1 - own, back + own
 
         times(left, first)
-        fronts[shard], backs[shard] = lax.fori_loop(0, count_ref[shard], second, (left, jnp.int32(0)))
-
-    def even(back, stride, most, so_far, send_at):
-        numbers = backs if back else fronts
+        front, back = lax.fori_loop(0, count_ref[shard], second, (left, jnp.int32(0)))
+        fronts[shard], backs[shard] = front, back
+        kept_fronts[shard], kept_backs[shard] = front, back
+
+    def late_spot(back, shard, i):
+        return (back * shards + shard) * late_room + i
+
+    def even(level, back, stride, most, so_far, send_at):
+        numbers, kept = (backs, kept_backs) if back else (fronts, kept_fronts)
 
         def weight(shard):
             return fronts[shard] + backs[shard] if back else fronts[shard]
@@ -280,28 +286,37 @@
         def decide(shard):
             partner = shard ^ stride
             excess = lax.div(jnp.maximum(weight(shard) - weight(partner), 0), jnp.int32(2))
-            spare = numbers[shard] if back else numbers[shard] - left_ref[shard]
+            spare = kept[shard] if back else kept[shard] - left_ref[shard]
             room = jnp.minimum(most, capacity - numbers[partner])
             sent_ref[shard] = jnp.minimum(excess, jnp.minimum(room, spare))
 
         def hand_over(shard):
             partner, sent = shard ^ stride, sent_ref[shard]
-            here, there = numbers[shard] - sent, numbers[partner]
+            here, there = kept[shard] - sent, numbers[partner]
+            there_late = there - kept[partner]
 
             def one(i):
-                old, new = spot(back, shard, here + i), spot(back, partner, there + i)
-                place_ref[new] = place_ref[old]
+                old = spot(back, shard, here + i)
 
                 @pl.when(shard == me)
                 def _():
                     send_ref[send_at + i] = source_ref[old]
 
-                source_ref[new] = so_far + i
+                if level == 0:
+                    new = spot(back, partner, there + i)
+                    place_ref[new] = place_ref[old]
+                    source_ref[new] = so_far + i
+                else:
+                    new = late_spot(back, partner, there_late + i)
+                    late_place_ref[new] = place_ref[old]
+                    late_source_ref[new] = so_far + i
 
             times(sent, one)
 
         def settle(shard):
-            numbers[shard] = numbers[shard] - sent_ref[shard] + sent_ref[shard ^ stride]
+            got = sent_ref[shard ^ stride]
+            numbers[shard] = numbers[shard] - sent_ref[shard] + got
+            kept[shard] = kept[shard] - sent_ref[shard] + (got if level == 0 else 0)
 
         for work in (decide, hand_over, settle):
             times(shards, work)
@@ -311,18 +326,19 @@
         front_count_ref[shard] = front
         length_ref[shard] = front + back
 
-        def copy(back, start):
+        def copy(count, places, sources, at, start):
             def one(i):
-                code_ref[shard * total + start + i] = place_ref[spot(back, shard, i)]
+                code_ref[shard * total + start + i] = places[at + i]
 
                 @pl.when(shard == me)
                 def _():
-                    order_ref[start + i] = source_ref[spot(back, shard, i)]
-
-            return one
-
-        times(front, copy(0, 0))
-        times(back, copy(1, front))
+                    order_ref[start + i] = sources[at + i]
+
+            times(count, one)
+
+        for back, start, number, kept in ((0, 0, front, kept_fronts[shard]), (1, front, back, kept_backs[shard])):
+            copy(kept, place_ref, source_ref, spot(back, shard, 0), start)
+            copy(number - kept, late_place_ref, late_source_ref, late_spot(back, shard, 0), start + kept)
 
     def clear(ref):
         def one(i):
@@ -334,10 +350,10 @@
     clear(send_ref)
     times(shards, build)
     so_far, send_at = capacity, 0
-    for stride, most_front, most_back in levels:
+    for level, (stride, most_front, most_back) in enumerate(levels):
         for back, most in ((0, most_front), (1, most_back)):
             if most:
-                even(back, stride, most, so_far, send_at)
+                even(level, back, stride, most, so_far, send_at)
             so_far, send_at = so_far + most, send_at + most
     times(shards, lay_out)
 
@@ -346,7 +362,8 @@
     shards, slots = index.shape
     smem = pl.BlockSpec(memory_space=pltpu.SMEM)
     sizes = [shards * total, shards, shards, total, sum(front + back for _, front, back in levels)]
-    scratch = [2 * shards * capacity, 2 * shards * capacity, shards, shards, shards]
+    late_room = max(sum(front + back for _, front, back in levels[1:]), 1)
+    scratch = [2 * shards * capacity] * 2 + [2 * shards * late_room] * 2 + [shards] * 5
     return pl.pallas_call(
         functools.partial(layout_kernel, levels, capacity),
         out_shape=[jax.ShapeDtypeStruct((size,), jnp.int32) for size in sizes],
@@ -413,14 +430,19 @@
     )
     codes = codes.reshape(shards, -1)
     sources = jnp.concatenate([fc1_tiles[0, 0, opening:], fc2_tiles[0, 0]], axis=0)
-    for stride, most_front, most_back in levels:
+    arrived = []
+    for level, (stride, most_front, most_back) in enumerate(levels):
         sending, sends = sends[: most_front + most_back], sends[most_front + most_back :]
-        arrived = lax.ppermute(
-            jnp.take(sources, sending, axis=0, mode="clip"),
-            "blk",
-            [(i, i ^ stride) for i in range(shards)],
+        arrived.append(
+            lax.ppermute(
+                jnp.take(sources, sending, axis=0, mode="clip"),
+                "blk",
+                [(i, i ^ stride) for i in range(shards)],
+            )
         )
-        sources = jnp.concatenate([sources, arrived], axis=0)
+        if level == 0:
+            sources = jnp.concatenate([sources, arrived.pop()], axis=0)
+    sources = jnp.concatenate([sources, *arrived], axis=0)
 
     tiles2a = gathered(jnp.take(sources, order[:late_from], axis=0, mode="clip"))
     tiles2b = gathered(jnp.take(sources, order[late_from:held], axis=0, mode="clip"))

time: 513 us -> 513 us (level)
  waiting for transfers between devices: 135 us -> 148 us
  local copies, waits for them, and re-layouts: 64 us -> 56.4 us
    all_gather x3, waiting for transfers between devices: 84.3 us -> 124 us  [gathered(): lax.all_gather(value, 'blk', axis=0, tiled=True)]
    ppermute x4, waiting for transfers between devices: 41.9 us -> 14.6 us  [on_device(): lax.ppermute(jnp.take(sources, sending, axis=0, mode='clip'), 'blk', [(i,...]
    unnamed x50 -> x47, local copies, waits for them, and re-layouts: 19.6 us -> 13.8 us
  transfers between devices with their start and end apart: 8 -> 8, of which waited for: 6 -> 6; matrix products, arithmetic and copies ran while one was open for 15% -> 13% of each run, Pallas kernels for 44% -> 44%
where the time goes in v2:
time: 513 us; the launch traced here: 512 us
  Pallas kernels  244 us (48%)
  waiting for transfers between devices  148 us (29%)
  local copies, waits for them, and re-layouts  56.4 us (11%)
  blocking collectives  27.9 us (5%)
  other arithmetic  17.2 us (3%)
  between operations  16.6 us (3%)
    all_gather x3, waiting for transfers between devices, gathered(): lax.all_gather(value, 'blk', axis=0, tiled=True)  124 us
    pallas_call x4, Pallas kernels, tile_pass(): pl.pallas_call(functools.partial(kernel, group), out_shape=out_shapes, gr...  116 us
    pallas_call x4, Pallas kernels, group_up(): pl.pallas_call(functools.partial(group_kernel, group, size, zero_row), ou...  90.2 us
    pallas_call x1, Pallas kernels, laid_out(): pl.pallas_call(functools.partial(layout_kernel, levels, capacity), out_sh...  37.1 us
    all_gather x1, blocking collectives, on_device(): meta = lax.all_gather(meta, 'blk', axis=0, tiled=True)  23.1 us
    ppermute x4, waiting for transfers between devices, on_device(): lax.ppermute(jnp.take(sources, sending, axis=0, mode='clip'), 'blk', [(i,...  14.6 us
    unnamed x47, local copies, waits for them, and re-layouts  13.8 us
    gather x4, local copies, waits for them, and re-layouts, on_device(): jnp.take(sources, sending, axis=0, mode='clip')  13.4 us
  transfers between devices with their start and end apart: 8, of which 6 were waited for; matrix products, arithmetic and copies ran while one was open for 13% of the time, Pallas kernels for 44%

profile of v2, /device:TPU:0, one launch (start us, length us, event | category | flops | bytes accessed | tf_op | source)
XLA Modules:
  0.0 511.9 jit_solution(4117154608370234323)
XLA Ops:
  6.5 3.6 slice.121
  11.6 23.1 %all-gather.4 = s32[16,1,204]{2,1,0:T(1,128)S(1)} all-gather(s32[1,1,204]{2,1,0:T(1,128)S(1)} %add_bitcast_fusion), channel_id=1, replica_groups=mesh['blk'=16,'ffn'=2] {'blk'}, dimensions={0}, use_global_device_ids=true | all-gather | bytes 13872 | tf_op jit(solution)/shard_map/all_gather | solution.py:416
  37.0 37.1 %shard_map.111 = (s32[4560]{0:T(1024)}, s32[16]{0:T(128)}, s32[16]{0:T(128)}, s32[285]{0:T(512)S(1)}, s32[55]{0:T(128)}) custom-call(s32[1616]{0:T(1024)} %reshape.137.index_ref, s32[1616]{0:T(1024)} %reshape.151.own_ref, s32[16]{0:T(128)} %get-tuple-element.285.count_ref, s32[16]{0:T(128)} %get-tuple-element.284.left_ref, s32[1]{0:T(128)} %bitcast.11.at_ref), custom_call_target="tpu_custom_call" | custom-call | bytes 25856 | tf_op jit(solution)/shard_map/pallas_call | solution.py:367
  76.9 2.4 pad_maximum_fusion.1
  79.3 4.0 gather_fusion.1
  83.7 2.4 constant_dynamic-update-slice_fusion.5
  86.0 1.9 constant_dynamic-update-slice_fusion.4
  88.9 4.1 pad_maximum_fusion
  93.0 3.2 gather_fusion.2
  96.4 3.1 gather_fusion.3
  99.6 3.2 gather_fusion.4
  103.2 2.2 constant_dynamic-update-slice_fusion.3
  105.4 11.0 %collective-permute-done.2 = bf16[12,128,128]{2,1,0:T(8,128)(2,1)S(1)} collective-permute-done((bf16[12,128,128]{2,1,0:T(8,128)(2,1)S(1)}, bf16[12,128,128]{2,1,0:T(8,128)(2,1)S(1)}, u32[]{:S(2)}, u32[]{:S(2)}) %collective-permute-start.2) | collective-permute-done | bytes 393248 | tf_op jit(solution)/shard_map/ppermute | solution.py:437
  117.2 2.6 collective-permute-done.3
  122.3 5.3 %gather_fusion.5 = bf16[69,128,128]{2,1,0:T(8,128)(2,1)} fusion(bf16[185,128,128]{2,1,0:T(8,128)(2,1)} %constant_dynamic-update-slice_fusion, s32[1024]{0:T(1024)S(1)} %pad_clamp_fusion.2), kind=kCustom, calls=%fused_computation.5 | custom fusion | bytes 4522260 | tf_op jit(solution)/shard_map/jit(_take)/gather | solution.py:447
  127.8 4.7 gather_fusion.6
  135.6 4.8 pmax.7
  144.7 2.8 copy.18
  148.9 3.5 fusion.7
  152.4 3.0 copy.19
  157.7 15.7 %shard_map.114 = (s32[1920]{0:T(1024)}, s32[4]{0:T(128)}) custom-call(s32[464]{0:T(512)} %reshape_reshape.14.row_ref, s32[464]{0:T(512)} %compare_select_fusion.1.col_ref), custom_call_target="tpu_custom_call" | custom-call | bytes 7424 | tf_op jit(solution)/shard_map/pallas_call | solution.py:61
  174.0 32.5 %shard_map.115 = (s32[3680]{0:T(1024)}, s32[4]{0:T(128)}) custom-call(s32[1152]{0:T(1024)} %reshape_reshape.15.row_ref, s32[1152]{0:T(1024)} %compare_select_fusion.col_ref), custom_call_target="tpu_custom_call" | custom-call | bytes 18432 | tf_op jit(solution)/shard_map/pallas_call | solution.py:61
  206.5 27.5 %shard_map.113 = (s32[3024]{0:T(1024)}, s32[2]{0:T(128)}) custom-call(s32[1104]{0:T(1024)} %reshape_reshape.13.row_ref, s32[1104]{0:T(1024)} %select_n.161.col_ref), custom_call_target="tpu_custom_call" | custom-call | bytes 17664 | tf_op jit(solution)/shard_map/pallas_call | solution.py:61
  234.1 45.8 %shard_map.116.sum_ref = f32[72,256,128]{2,1,0:T(8,128)} custom-call(s32[3680]{0:T(1024)} %get-tuple-element.274.field_ref, s32[4]{0:T(128)} %get-tuple-element.275.count_ref, s32[1]{0:T(128)} %bitcast.15.at_ref, bf16[37,256,128]{2,1,0:T(8,128)(2,1)} %pad.4.x_ref, bf16[16,72,128,128]{3,2,1,0:T(8,128)(2,1)} %bitcast.55, f32[72,1,128]{2,1,0:T(1,128)} %bitcast.59), custom_call_target="tpu_custom_call" | custom-call | flops 19327352832 | bytes 37748736 | tf_op jit(solution)/shard_map/pallas_call | solution.py:211
  279.9 113.6 %all-gather.12.cloned.1.call-done = bf16[1104,128,128]{2,1,0:T(8,128)(2,1)} async-done(((bf16[69,128,128]{2,1,0:T(8,128)(2,1)}), bf16[1104,128,128]{2,1,0:T(8,128)(2,1)}) %all-gather.12.cloned.1.call-update) | async-done | bytes 36175888 | tf_op jit(solution)/shard_map/all_gather | solution.py:412
  393.5 17.9 %shard_map.117.x_ref = bf16[73,256,128]{2,1,0:T(8,128)(2,1)S(1)} custom-call(s32[1920]{0:T(1024)} %get-tuple-element.269.field_ref, s32[4]{0:T(128)} %get-tuple-element.270.count_ref, s32[1]{0:T(128)} %bitcast.15.at_ref, bf16[37,256,128]{2,1,0:T(8,128)(2,1)} %pad.4.x_ref, bf16[16,69,128,128]{3,2,1,0:T(8,128)(2,1)} %bitcast.37, ...), custom_call_target="tpu_custom_call" | custom-call | flops 7784628224 | bytes 15204352 | tf_op jit(solution)/shard_map/pallas_call | solution.py:211
  411.4 35.1 %shard_map.118 = (f32[36,256,128]{2,1,0:T(8,128)}, bf16[256,4608]{1,0:T(8,128)(2,1)}) custom-call(s32[3024]{0:T(1024)} %get-tuple-element.267.field_ref, s32[2]{0:T(128)} %get-tuple-element.268.count_ref, s32[1]{0:T(128)} %bitcast.15.at_ref, bf16[73,256,128]{2,1,0:T(8,128)(2,1)S(1)} %shard_map.117.x_ref, bf16[16,69,128,128]{3,2,1,0:T(8,128)(2,1)} %bitcast.38), custom_call_target="tpu_custom_call" | custom-call | flops 18522046464 | bytes 36175872 | tf_op jit(solution)/shard_map/pallas_call | solution.py:211
  452.8 14.5 %shard_map.112 = (s32[1728]{0:T(1024)}, s32[4]{0:T(128)}) custom-call(s32[528]{0:T(1024)} %reshape_reshape.12.row_ref, s32[528]{0:T(1024)} %select_n.157.col_ref), custom_call_target="tpu_custom_call" | custom-call | bytes 8448 | tf_op jit(solution)/shard_map/pallas_call | solution.py:61
  467.2 9.0 %collective-permute-done.5 = bf16[256,2304]{1,0:T(8,128)(2,1)S(1)} collective-permute-done((bf16[256,2304]{1,0:T(8,128)(2,1)S(1)}, bf16[256,2304]{1,0:T(8,128)(2,1)S(1)}, u32[]{:S(2)}, u32[]{:S(2)}) %collective-permute-start.5) | collective-permute-done | bytes 1179680 | tf_op jit(solution)/shard_map/ppermute | solution.py:517
  476.4 10.2 %all-gather.16.cloned.1.call-done = bf16[528,128,128]{2,1,0:T(8,128)(2,1)} async-done(((bf16[33,128,128]{2,1,0:T(8,128)(2,1)}), bf16[528,128,128]{2,1,0:T(8,128)(2,1)}) %all-gather.16.cloned.1.call-update) | async-done | bytes 17301520 | tf_op jit(solution)/shard_map/all_gather | solution.py:412
  486.6 17.7 %conditional.1 = (bf16[256,2304]{1,0:T(8,128)(2,1)S(1)}) conditional(s32[]{:T(128)} %convert_element_type.29, (s32[]{:T(128)}, s32[1728]{0:T(1024)}, s32[4]{0:T(128)}, bf16[73,256,128]{2,1,0:T(8,128)(2,1)}, bf16[16,33,128,128]{3,2,1,0:T(8,128)(2,1)}, /*index=5*/f32[36,256,128]{2,1,0:T(8,128)}, bf16[256,4608]{1,0:T(8,128)(2,1)}, ...), branch_computations={%region_6.7_spmd, %region_7.10_spmd} | conditional | flops 15571631104 | bytes 88066664 | solution.py:591
  486.6 17.7 %branch_0_fun.1 = bf16[256,2304]{1,0:T(8,128)(2,1)S(1)} custom-call(s32[1728]{0:T(1024)} %get-tuple-element.197.field_ref, s32[4]{0:T(128)} %get-tuple-element.198.count_ref, s32[1]{0:T(128)} %bitcast.at_ref, bf16[73,256,128]{2,1,0:T(8,128)(2,1)} %get-tuple-element.200.x_ref, bf16[16,33,128,128]{3,2,1,0:T(8,128)(2,1)} %get-tuple-element.201.w_ref, ...), custom_call_target="tpu_custom_call" | custom-call | flops 8858370048 | bytes 17301504 | tf_op jit(solution)/shard_map/cond/branch_0_fun/pallas_call | solution.py:211
  (125 shorter events, 27.9 us)
Async XLA Ops:
  6.5 4.9 copy-start.17
  6.5 4.9 copy-start.18
  6.5 227.5 %all-gather.14.cloned.1.call-start = ((), (), s32[]{:S(2)}) async-start(), calls=%async_computation.1 | async-start | bytes 40108032 | tf_op jit(solution)/shard_map/all_gather | solution.py:412
  6.5 70.4 %copy-start = (bf16[1,1,101,128,128]{4,3,2,1,0:T(8,128)(2,1)S(1)}, bf16[1,1,101,128,128]{4,3,2,1,0:T(8,128)(2,1)}, u32[]{:S(2)}) copy-start(bf16[1,1,101,128,128]{4,3,2,1,0:T(8,128)(2,1)} %param.22) | copy-start | bytes 9928708
  10.1 383.3 %all-gather.12.cloned.1.call-start = ((), (), s32[]{:S(2)}) async-start(), calls=%async_computation | async-start | bytes 38436864 | tf_op jit(solution)/shard_map/all_gather | solution.py:412
  74.1 53.6 %copy-start.20 = (s32[285]{0:T(512)}, s32[285]{0:T(512)S(1)}, u32[]{:S(2)}) copy-start(s32[285]{0:T(512)S(1)} %get-tuple-element.273) | copy-start | bytes 3424
  76.0 0.9 copy-start.1
  76.9 6.6 %copy-start.16 = (s32[55]{0:T(128)S(1)}, s32[55]{0:T(128)}, u32[]{:S(2)}) copy-start(s32[55]{0:T(128)} %get-tuple-element.272) | copy-start | bytes 664
  83.3 4.6 collective-permute-start.1
  83.7 5.2 %copy-start.2 = (bf16[29,128,128]{2,1,0:T(8,128)(2,1)S(1)}, bf16[29,128,128]{2,1,0:T(8,128)(2,1)}, u32[]{:S(2)}) copy-start(bf16[29,128,128]{2,1,0:T(8,128)(2,1)} %copy-done.1) | copy-start | bytes 2850820
  87.9 0.9 copy-start.4
  96.2 20.2 %collective-permute-start.2 = (bf16[12,128,128]{2,1,0:T(8,128)(2,1)S(1)}, bf16[12,128,128]{2,1,0:T(8,128)(2,1)S(1)}, u32[]{:S(2)}, u32[]{:S(2)}) collective-permute-start(bf16[12,128,128]{2,1,0:T(8,128)(2,1)S(1)} %gather_fusion.2), channel_id=1, source_target_pairs={{0,4},{2,6},{4,0},{6,2},{8,12},{10,14},{12,8},{14,10},{16,20},{18,... | collective-permute-start | bytes 1179656 | tf_op jit(solution)/shard_map/ppermute | solution.py:437
  99.5 20.3 %collective-permute-start.3 = (bf16[9,128,128]{2,1,0:T(8,128)(2,1)S(1)}, bf16[9,128,128]{2,1,0:T(8,128)(2,1)S(1)}, u32[]{:S(2)}, u32[]{:S(2)}) collective-permute-start(bf16[9,128,128]{2,1,0:T(8,128)(2,1)S(1)} %gather_fusion.3), channel_id=1, source_target_pairs={{0,8},{2,10},{4,12},{6,14},{8,0},{10,2},{12,4},{14,6},{16,24},{18,... | collective-permute-start | bytes 884744 | tf_op jit(solution)/shard_map/ppermute | solution.py:437
  102.7 18.9 %collective-permute-start.4 = (bf16[6,128,128]{2,1,0:T(8,128)(2,1)S(1)}, bf16[6,128,128]{2,1,0:T(8,128)(2,1)S(1)}, u32[]{:S(2)}, u32[]{:S(2)}) collective-permute-start(bf16[6,128,128]{2,1,0:T(8,128)(2,1)S(1)} %gather_fusion.4), channel_id=1, source_target_pairs={{0,16},{2,18},{4,20},{6,22},{8,24},{10,26},{12,28},{14,30},{16,0},... | collective-permute-start | bytes 589832 | tf_op jit(solution)/shard_map/ppermute | solution.py:437
  122.3 10.2 %copy-start.15 = (s32[16]{0:T(128)S(1)}, s32[16]{0:T(128)}, u32[]{:S(2)}) copy-start(s32[16]{0:T(128)} %get-tuple-element.262) | copy-start | bytes 196
  122.3 10.9 %copy-start.14 = (s32[16]{0:T(128)S(1)}, s32[16]{0:T(128)}, u32[]{:S(2)}) copy-start(s32[16]{0:T(128)} %get-tuple-element.261) | copy-start | bytes 196
  122.3 19.0 %copy-start.8 = (s32[4560]{0:T(1024)S(1)}, s32[4560]{0:T(1024)}, u32[]{:S(2)}) copy-start(s32[4560]{0:T(1024)} %get-tuple-element.264) | copy-start | bytes 54724
  122.3 20.9 %copy-start.12 = (s32[16]{0:T(128)S(1)}, s32[16]{0:T(128)}, u32[]{:S(2)}) copy-start(s32[16]{0:T(128)} %get-tuple-element.284.left_ref) | copy-start | bytes 196
  127.6 359.0 %all-gather.16.cloned.1.call-start = ((), (), s32[]{:S(2)}) async-start(), calls=%async_computation.2 | async-start | bytes 18382848 | tf_op jit(solution)/shard_map/all_gather | solution.py:412
  141.4 2.6 copy-start.5
  144.7 4.2 copy-start.9
  144.7 4.2 copy-start.10
  411.3 35.2 %copy-start.3 = (bf16[73,256,128]{2,1,0:T(8,128)(2,1)}, bf16[73,256,128]{2,1,0:T(8,128)(2,1)S(1)}, u32[]{:S(2)}) copy-start(bf16[73,256,128]{2,1,0:T(8,128)(2,1)S(1)} %shard_map.117.x_ref) | copy-start | bytes 14352388
  411.4 38.1 %copy-start.11 = (f32[2304]{0:T(1024)S(1)}, f32[2304]{0:T(1024)}, u32[]{:S(2)}) copy-start(f32[2304]{0:T(1024)} %param.25) | copy-start | bytes 27652
  411.4 38.7 %copy-start.6 = (s32[16,285]{1,0:T(8,128)S(1)}, s32[16,285]{1,0:T(8,128)}, u32[]{:S(2)}) copy-start(s32[16,285]{1,0:T(8,128)} %copy-done.5) | copy-start | bytes 54724
  411.4 40.2 %copy-start.13 = (s32[3]{0:T(128)S(1)}, s32[3]{0:T(128)}, u32[]{:S(2)}) copy-start(s32[3]{0:T(128)} %pmax.7) | copy-start | bytes 40
  447.9 28.4 %collective-permute-start.5 = (bf16[256,2304]{1,0:T(8,128)(2,1)S(1)}, bf16[256,2304]{1,0:T(8,128)(2,1)S(1)}, u32[]{:S(2)}, u32[]{:S(2)}) collective-permute-start(bf16[256,2304]{1,0:T(8,128)(2,1)S(1)} %constant_dynamic-slice_fusion.1), channel_id=1, source_target_pairs={{0,1},{1,0},{2,3},{3,2},{4,5},{5,4},{6,7},{7,6},{8,9},{9,8},{10,11... | collective-permute-start | bytes 3538952 | tf_op jit(solution)/shard_map/ppermute | solution.py:517
  504.3 1.0 copy-start.21
Sparse Core Ops, SparseCore 0:
  10.2 201.1 all-gather.13
  213.0 180.3 all-gather.11
  395.1 91.5 all-gather.15

commit v3 on v2

--- a/solution.py
+++ b/solution.py
@@ -397,13 +397,13 @@
     share = width // ffn_size
     blk, ffn = lax.axis_index("blk"), lax.axis_index("ffn")
     aligned = share % side == 0
-    opening = slots * 5 // 7
+    opening = slots * 7 // 11
     rest = slots - opening
-    held = slots + slots // 100
+    held = slots + slots // 14
     late_from = held - slots // 3
     levels = [
         (stride, slots // most, max(slots // least, 1))
-        for stride, most, least in ((1, 6, 8), (2, 16, 16), (4, 32, 16), (8, slots + 1, 16))
+        for stride, most, least in ((1, 4, 5), (2, 14, 16), (4, 25, 16), (8, 50, 16))
         if shards % (2 * stride) == 0
     ]
     slot_ids = jnp.arange(slots, dtype=jnp.int32)

time: 513 us -> 511 us (level)
  waiting for transfers between devices: 148 us -> 135 us
  Pallas kernels: 244 us -> 251 us
    all_gather x3, waiting for transfers between devices: 124 us -> 106 us  [gathered(): lax.all_gather(value, 'blk', axis=0, tiled=True)]
    unnamed x47 -> x49, local copies, waits for them, and re-layouts: 13.8 us -> 14.9 us
  transfers between devices with their start and end apart: 8 -> 8, of which waited for: 6 -> 6; matrix products, arithmetic and copies ran while one was open for 13% -> 14% of each run, Pallas kernels for 44% -> 46%
where the time goes in v3:
time: 511 us; the launch traced here: 509 us
  Pallas kernels  251 us (49%)
  waiting for transfers between devices  135 us (26%)
  local copies, waits for them, and re-layouts  58.9 us (12%)
  blocking collectives  28 us (5%)
  other arithmetic  17.8 us (3%)
  between operations  17 us (3%)
    pallas_call x4, Pallas kernels, tile_pass(): pl.pallas_call(functools.partial(kernel, group), out_shape=out_shapes, gr...  119 us
    all_gather x3, waiting for transfers between devices, gathered(): lax.all_gather(value, 'blk', axis=0, tiled=True)  106 us
    pallas_call x4, Pallas kernels, group_up(): pl.pallas_call(functools.partial(group_kernel, group, size, zero_row), ou...  91.9 us
    pallas_call x1, Pallas kernels, laid_out(): pl.pallas_call(functools.partial(layout_kernel, levels, capacity), out_sh...  40.5 us
    all_gather x1, blocking collectives, on_device(): meta = lax.all_gather(meta, 'blk', axis=0, tiled=True)  23.1 us
    ppermute x4, waiting for transfers between devices, on_device(): lax.ppermute(jnp.take(sources, sending, axis=0, mode='clip'), 'blk', [(i,...  18.1 us
    unnamed x49, local copies, waits for them, and re-layouts  14.9 us
    gather x4, local copies, waits for them, and re-layouts, on_device(): jnp.take(sources, sending, axis=0, mode='clip')  14.7 us
  transfers between devices with their start and end apart: 8, of which 6 were waited for; matrix products, arithmetic and copies ran while one was open for 14% of the time, Pallas kernels for 46%

profile of v3, /device:TPU:0, one launch (start us, length us, event | category | flops | bytes accessed | tf_op | source)
XLA Modules:
  0.0 508.6 jit_solution(13833322928204936482)
XLA Ops:
  6.5 3.2 slice.121
  11.5 23.1 %all-gather.4 = s32[16,1,204]{2,1,0:T(1,128)S(1)} all-gather(s32[1,1,204]{2,1,0:T(1,128)S(1)} %add_bitcast_fusion), channel_id=1, replica_groups=mesh['blk'=16,'ffn'=2] {'blk'}, dimensions={0}, use_global_device_ids=true | all-gather | bytes 13872 | tf_op jit(solution)/shard_map/all_gather | solution.py:416
  36.8 40.5 %shard_map.111 = (s32[4816]{0:T(1024)}, s32[16]{0:T(128)}, s32[16]{0:T(128)}, s32[301]{0:T(512)S(1)}, s32[76]{0:T(128)}) custom-call(s32[1616]{0:T(1024)} %reshape.137.index_ref, s32[1616]{0:T(1024)} %reshape.151.own_ref, s32[16]{0:T(128)} %get-tuple-element.285.count_ref, s32[16]{0:T(128)} %get-tuple-element.284.left_ref, s32[1]{0:T(128)} %bitcast.11.at_ref), custom_call_target="tpu_custom_call" | custom-call | bytes 25856 | tf_op jit(solution)/shard_map/pallas_call | solution.py:367
  80.7 2.5 pad_maximum_fusion.1
  83.2 4.5 gather_fusion.1
  88.0 2.5 constant_dynamic-update-slice_fusion.5
  93.6 4.6 pad_maximum_fusion
  98.2 3.3 gather_fusion.2
  101.7 3.4 gather_fusion.3
  105.2 3.4 gather_fusion.4
  109.0 2.7 constant_dynamic-update-slice_fusion.3
  111.7 11.5 %collective-permute-done.2 = bf16[13,128,128]{2,1,0:T(8,128)(2,1)S(1)} collective-permute-done((bf16[13,128,128]{2,1,0:T(8,128)(2,1)S(1)}, bf16[13,128,128]{2,1,0:T(8,128)(2,1)S(1)}, u32[]{:S(2)}, u32[]{:S(2)}) %collective-permute-start.2) | collective-permute-done | bytes 426016 | tf_op jit(solution)/shard_map/ppermute | solution.py:437
  124.0 4.1 collective-permute-done.3
  128.9 2.5 collective-permute-done.4
  132.1 5.6 %gather_fusion.5 = bf16[75,128,128]{2,1,0:T(8,128)(2,1)} fusion(bf16[214,128,128]{2,1,0:T(8,128)(2,1)} %constant_dynamic-update-slice_fusion, s32[1024]{0:T(1024)S(1)} %pad_clamp_fusion.2), kind=kCustom, calls=%fused_computation.5 | custom fusion | bytes 4915500 | tf_op jit(solution)/shard_map/jit(_take)/gather | solution.py:447
  137.9 4.8 gather_fusion.6
  145.9 4.8 pmax.7
  154.8 2.8 copy.18
  159.0 3.5 fusion.7
  162.5 3.1 copy.19
  167.9 18.8 %shard_map.114 = (s32[2240]{0:T(1024)}, s32[4]{0:T(128)}) custom-call(s32[592]{0:T(1024)} %reshape_reshape.14.row_ref, s32[592]{0:T(1024)} %compare_select_fusion.1.col_ref), custom_call_target="tpu_custom_call" | custom-call | bytes 9472 | tf_op jit(solution)/shard_map/pallas_call | solution.py:61
  187.3 28.8 %shard_map.115 = (s32[3360]{0:T(1024)}, s32[4]{0:T(128)}) custom-call(s32[1024]{0:T(1024)} %reshape_reshape.15.row_ref, s32[1024]{0:T(1024)} %compare_select_fusion.col_ref), custom_call_target="tpu_custom_call" | custom-call | bytes 16384 | tf_op jit(solution)/shard_map/pallas_call | solution.py:61
  216.2 29.8 %shard_map.113 = (s32[3312]{0:T(1024)}, s32[2]{0:T(128)}) custom-call(s32[1200]{0:T(1024)} %reshape_reshape.13.row_ref, s32[1200]{0:T(1024)} %select_n.161.col_ref), custom_call_target="tpu_custom_call" | custom-call | bytes 19200 | tf_op jit(solution)/shard_map/pallas_call | solution.py:61
  246.0 43.6 %shard_map.116.sum_ref = f32[72,256,128]{2,1,0:T(8,128)} custom-call(s32[3360]{0:T(1024)} %get-tuple-element.274.field_ref, s32[4]{0:T(128)} %get-tuple-element.275.count_ref, s32[1]{0:T(128)} %bitcast.15.at_ref, bf16[37,256,128]{2,1,0:T(8,128)(2,1)} %pad.4.x_ref, bf16[16,64,128,128]{3,2,1,0:T(8,128)(2,1)} %bitcast.59, f32[72,1,128]{2,1,0:T(1,128)} %bitcast.63), custom_call_target="tpu_custom_call" | custom-call | flops 17179869184 | bytes 33554432 | tf_op jit(solution)/shard_map/pallas_call | solution.py:211
  289.6 100.6 %all-gather.12.cloned.1.call-done = bf16[1200,128,128]{2,1,0:T(8,128)(2,1)} async-done(((bf16[75,128,128]{2,1,0:T(8,128)(2,1)}), bf16[1200,128,128]{2,1,0:T(8,128)(2,1)}) %all-gather.12.cloned.1.call-update) | async-done | bytes 39321616 | tf_op jit(solution)/shard_map/all_gather | solution.py:412
  390.2 21.9 %shard_map.117.x_ref = bf16[73,256,128]{2,1,0:T(8,128)(2,1)S(1)} custom-call(s32[2240]{0:T(1024)} %get-tuple-element.269.field_ref, s32[4]{0:T(128)} %get-tuple-element.270.count_ref, s32[1]{0:T(128)} %bitcast.15.at_ref, bf16[37,256,128]{2,1,0:T(8,128)(2,1)} %pad.4.x_ref, bf16[16,75,128,128]{3,2,1,0:T(8,128)(2,1)} %bitcast.40, ...), custom_call_target="tpu_custom_call" | custom-call | flops 9932111872 | bytes 19398656 | tf_op jit(solution)/shard_map/pallas_call | solution.py:211
  412.2 35.9 %shard_map.118 = (f32[36,256,128]{2,1,0:T(8,128)}, bf16[256,4608]{1,0:T(8,128)(2,1)}) custom-call(s32[3312]{0:T(1024)} %get-tuple-element.267.field_ref, s32[2]{0:T(128)} %get-tuple-element.268.count_ref, s32[1]{0:T(128)} %bitcast.15.at_ref, bf16[73,256,128]{2,1,0:T(8,128)(2,1)S(1)} %shard_map.117.x_ref, bf16[16,75,128,128]{3,2,1,0:T(8,128)(2,1)} %bitcast.41), custom_call_target="tpu_custom_call" | custom-call | flops 20132659200 | bytes 39321600 | tf_op jit(solution)/shard_map/pallas_call | solution.py:211
  453.0 14.5 %shard_map.112 = (s32[1728]{0:T(1024)}, s32[4]{0:T(128)}) custom-call(s32[528]{0:T(1024)} %reshape_reshape.12.row_ref, s32[528]{0:T(1024)} %select_n.157.col_ref), custom_call_target="tpu_custom_call" | custom-call | bytes 8448 | tf_op jit(solution)/shard_map/pallas_call | solution.py:61
  467.4 10.2 %collective-permute-done.5 = bf16[256,2304]{1,0:T(8,128)(2,1)S(1)} collective-permute-done((bf16[256,2304]{1,0:T(8,128)(2,1)S(1)}, bf16[256,2304]{1,0:T(8,128)(2,1)S(1)}, u32[]{:S(2)}, u32[]{:S(2)}) %collective-permute-start.5) | collective-permute-done | bytes 1179680 | tf_op jit(solution)/shard_map/ppermute | solution.py:517
  477.7 5.7 %all-gather.16.cloned.1.call-done = bf16[528,128,128]{2,1,0:T(8,128)(2,1)} async-done(((bf16[33,128,128]{2,1,0:T(8,128)(2,1)}), bf16[528,128,128]{2,1,0:T(8,128)(2,1)}) %all-gather.16.cloned.1.call-update) | async-done | bytes 17301520 | tf_op jit(solution)/shard_map/all_gather | solution.py:412
  483.4 17.7 %conditional.1 = (bf16[256,2304]{1,0:T(8,128)(2,1)S(1)}) conditional(s32[]{:T(128)} %convert_element_type.29, (s32[]{:T(128)}, s32[1728]{0:T(1024)}, s32[4]{0:T(128)}, bf16[73,256,128]{2,1,0:T(8,128)(2,1)}, bf16[16,33,128,128]{3,2,1,0:T(8,128)(2,1)}, /*index=5*/f32[36,256,128]{2,1,0:T(8,128)}, bf16[256,4608]{1,0:T(8,128)(2,1)}, ...), branch_computations={%region_6.7_spmd, %region_7.10_spmd} | conditional | flops 15571632128 | bytes 88068552 | solution.py:591
  483.4 17.6 %branch_0_fun.1 = bf16[256,2304]{1,0:T(8,128)(2,1)S(1)} custom-call(s32[1728]{0:T(1024)} %get-tuple-element.197.field_ref, s32[4]{0:T(128)} %get-tuple-element.198.count_ref, s32[1]{0:T(128)} %bitcast.at_ref, bf16[73,256,128]{2,1,0:T(8,128)(2,1)} %get-tuple-element.200.x_ref, bf16[16,33,128,128]{3,2,1,0:T(8,128)(2,1)} %get-tuple-element.201.w_ref, ...), custom_call_target="tpu_custom_call" | custom-call | flops 8858370048 | bytes 17301504 | tf_op jit(solution)/shard_map/cond/branch_0_fun/pallas_call | solution.py:211
  (125 shorter events, 27.8 us)
Async XLA Ops:
  6.5 4.8 copy-start.17
  6.5 4.8 copy-start.18
  6.5 239.4 %all-gather.14.cloned.1.call-start = ((), (), s32[]{:S(2)}) async-start(), calls=%async_computation.1 | async-start | bytes 35651584 | tf_op jit(solution)/shard_map/all_gather | solution.py:412
  9.7 71.0 %copy-start = (bf16[1,1,101,128,128]{4,3,2,1,0:T(8,128)(2,1)S(1)}, bf16[1,1,101,128,128]{4,3,2,1,0:T(8,128)(2,1)}, u32[]{:S(2)}) copy-start(bf16[1,1,101,128,128]{4,3,2,1,0:T(8,128)(2,1)} %param.22) | copy-start | bytes 9928708
  9.7 380.5 %all-gather.12.cloned.1.call-start = ((), (), s32[]{:S(2)}) async-start(), calls=%async_computation | async-start | bytes 41779200 | tf_op jit(solution)/shard_map/all_gather | solution.py:412
  77.4 60.4 %copy-start.20 = (s32[301]{0:T(512)}, s32[301]{0:T(512)S(1)}, u32[]{:S(2)}) copy-start(s32[301]{0:T(512)S(1)} %get-tuple-element.273) | copy-start | bytes 3616
  79.6 1.1 copy-start.1
  80.7 7.1 %copy-start.16 = (s32[76]{0:T(128)S(1)}, s32[76]{0:T(128)}, u32[]{:S(2)}) copy-start(s32[76]{0:T(128)} %get-tuple-element.272) | copy-start | bytes 916
  87.7 4.7 collective-permute-start.1
  90.5 3.1 copy-start.2
  92.4 1.2 copy-start.3
  101.5 21.7 %collective-permute-start.2 = (bf16[13,128,128]{2,1,0:T(8,128)(2,1)S(1)}, bf16[13,128,128]{2,1,0:T(8,128)(2,1)S(1)}, u32[]{:S(2)}, u32[]{:S(2)}) collective-permute-start(bf16[13,128,128]{2,1,0:T(8,128)(2,1)S(1)} %gather_fusion.2), channel_id=1, source_target_pairs={{0,4},{2,6},{4,0},{6,2},{8,12},{10,14},{12,8},{14,10},{16,20},{18,... | collective-permute-start | bytes 1277960 | tf_op jit(solution)/shard_map/ppermute | solution.py:437
  105.1 23.1 %collective-permute-start.3 = (bf16[10,128,128]{2,1,0:T(8,128)(2,1)S(1)}, bf16[10,128,128]{2,1,0:T(8,128)(2,1)S(1)}, u32[]{:S(2)}, u32[]{:S(2)}) collective-permute-start(bf16[10,128,128]{2,1,0:T(8,128)(2,1)S(1)} %gather_fusion.3), channel_id=1, source_target_pairs={{0,8},{2,10},{4,12},{6,14},{8,0},{10,2},{12,4},{14,6},{16,24},{18,... | collective-permute-start | bytes 983048 | tf_op jit(solution)/shard_map/ppermute | solution.py:437
  108.6 22.8 %collective-permute-start.4 = (bf16[8,128,128]{2,1,0:T(8,128)(2,1)S(1)}, bf16[8,128,128]{2,1,0:T(8,128)(2,1)S(1)}, u32[]{:S(2)}, u32[]{:S(2)}) collective-permute-start(bf16[8,128,128]{2,1,0:T(8,128)(2,1)S(1)} %gather_fusion.4), channel_id=1, source_target_pairs={{0,16},{2,18},{4,20},{6,22},{8,24},{10,26},{12,28},{14,30},{16,0},... | collective-permute-start | bytes 786440 | tf_op jit(solution)/shard_map/ppermute | solution.py:437
  137.7 5.0 copy-start.15
  137.7 5.7 %copy-start.14 = (s32[16]{0:T(128)S(1)}, s32[16]{0:T(128)}, u32[]{:S(2)}) copy-start(s32[16]{0:T(128)} %get-tuple-element.261) | copy-start | bytes 196
  137.7 13.8 %copy-start.8 = (s32[4816]{0:T(1024)S(1)}, s32[4816]{0:T(1024)}, u32[]{:S(2)}) copy-start(s32[4816]{0:T(1024)} %get-tuple-element.264) | copy-start | bytes 57796
  137.7 15.6 %copy-start.12 = (s32[16]{0:T(128)S(1)}, s32[16]{0:T(128)}, u32[]{:S(2)}) copy-start(s32[16]{0:T(128)} %get-tuple-element.284.left_ref) | copy-start | bytes 196
  137.7 345.7 %all-gather.16.cloned.1.call-start = ((), (), s32[]{:S(2)}) async-start(), calls=%async_computation.2 | async-start | bytes 18382848 | tf_op jit(solution)/shard_map/all_gather | solution.py:412
  151.6 2.5 copy-start.5
  157.7 1.3 copy-start.9
  157.7 1.3 copy-start.10
  412.1 35.9 %copy-start.4 = (bf16[73,256,128]{2,1,0:T(8,128)(2,1)}, bf16[73,256,128]{2,1,0:T(8,128)(2,1)S(1)}, u32[]{:S(2)}) copy-start(bf16[73,256,128]{2,1,0:T(8,128)(2,1)S(1)} %shard_map.117.x_ref) | copy-start | bytes 14352388
  412.1 37.3 %copy-start.11 = (f32[2304]{0:T(1024)S(1)}, f32[2304]{0:T(1024)}, u32[]{:S(2)}) copy-start(f32[2304]{0:T(1024)} %param.25) | copy-start | bytes 27652
  412.2 37.9 %copy-start.6 = (s32[16,301]{1,0:T(8,128)S(1)}, s32[16,301]{1,0:T(8,128)}, u32[]{:S(2)}) copy-start(s32[16,301]{1,0:T(8,128)} %copy-done.5) | copy-start | bytes 57796
  412.2 39.5 %copy-start.13 = (s32[3]{0:T(128)S(1)}, s32[3]{0:T(128)}, u32[]{:S(2)}) copy-start(s32[3]{0:T(128)} %pmax.7) | copy-start | bytes 40
  449.4 28.2 %collective-permute-start.5 = (bf16[256,2304]{1,0:T(8,128)(2,1)S(1)}, bf16[256,2304]{1,0:T(8,128)(2,1)S(1)}, u32[]{:S(2)}, u32[]{:S(2)}) collective-permute-start(bf16[256,2304]{1,0:T(8,128)(2,1)S(1)} %constant_dynamic-slice_fusion.1), channel_id=1, source_target_pairs={{0,1},{1,0},{2,3},{3,2},{4,5},{5,4},{6,7},{7,6},{8,9},{9,8},{10,11... | collective-permute-start | bytes 3538952 | tf_op jit(solution)/shard_map/ppermute | solution.py:517
  501.1 1.0 copy-start.21
Sparse Core Ops, SparseCore 0:
  9.9 183.4 all-gather.13
  194.9 195.2 all-gather.11
  391.8 91.5 all-gather.15

commit v4 on v3

--- a/solution.py
+++ b/solution.py
@@ -9,7 +9,7 @@
 
 UNROLL = 8
 VMEM_BYTES = 56 * 1024 * 1024
-LAST_VMEM_BYTES = 26 * 1024 * 1024
+LAST_VMEM_BYTES = 36 * 1024 * 1024
 
 
 def group_kernel(group, size, zero_row, row_ref, col_ref, field_ref, count_ref, fill_ref, open_ref):
@@ -400,7 +400,7 @@
     opening = slots * 7 // 11
     rest = slots - opening
     held = slots + slots // 14
-    late_from = held - slots // 3
+    late_from = held - slots * 8 // 25
     levels = [
         (stride, slots // most, max(slots // least, 1))
         for stride, most, least in ((1, 4, 5), (2, 14, 16), (4, 25, 16), (8, 50, 16))
@@ -551,7 +551,7 @@
 
     share_blocks = share // side
     last_rows, last_cols = last_codes // second_blocks, last_codes % second_blocks % share_blocks
-    last_plan = planned(last_rows, last_cols, last_own, share_blocks, first_blocks, 4, 4)
+    last_plan = planned(last_rows, last_cols, last_own, share_blocks, first_blocks, 2, 4)
     bias_row = fc2_bias.reshape(1, share)
     last_plan, branch, bias_row = lax.optimization_barrier((last_plan, branch, bias_row))
     last_pass = functools.partial(
@@ -579,7 +579,7 @@
         ],
         out_shapes=[jax.ShapeDtypeStruct((token_rows, share), jnp.bfloat16)],
         blocks=share_blocks,
-        steps=4,
+        steps=2,
         group=4,
         vmem=LAST_VMEM_BYTES,
         plan=last_plan,

time: 511 us -> 546 us (1.068)
  waiting for transfers between devices: 135 us -> 174 us
  Pallas kernels: 251 us -> 245 us
    all_gather x3, waiting for transfers between devices: 106 us -> 145 us  [gathered(): lax.all_gather(value, 'blk', axis=0, tiled=True)]
    unnamed x49 -> x51, local copies, waits for them, and re-layouts: 14.9 us -> 15.5 us
  transfers between devices with their start and end apart: 8 -> 8, of which waited for: 6 -> 6; matrix products, arithmetic and copies ran while one was open for 14% -> 13% of each run, Pallas kernels for 46% -> 42%
where the time goes in v4:
time: 546 us; the launch traced here: 544 us
  Pallas kernels  245 us (45%)
  waiting for transfers between devices  174 us (32%)
  local copies, waits for them, and re-layouts  58.6 us (11%)
  blocking collectives  28.6 us (5%)
  other arithmetic  19.2 us (4%)
  between operations  16.9 us (3%)
    all_gather x3, waiting for transfers between devices, gathered(): lax.all_gather(value, 'blk', axis=0, tiled=True)  145 us
    pallas_call x4, Pallas kernels, tile_pass(): pl.pallas_call(functools.partial(kernel, group), out_shape=out_shapes, gr...  115 us
    pallas_call x4, Pallas kernels, group_up(): pl.pallas_call(functools.partial(group_kernel, group, size, zero_row), ou...  91 us
    pallas_call x1, Pallas kernels, laid_out(): pl.pallas_call(functools.partial(layout_kernel, levels, capacity), out_sh...  38.7 us
    all_gather x1, blocking collectives, on_device(): meta = lax.all_gather(meta, 'blk', axis=0, tiled=True)  23.1 us
    ppermute x4, waiting for transfers between devices, on_device(): lax.ppermute(jnp.take(sources, sending, axis=0, mode='clip'), 'blk', [(i,...  18.1 us
    unnamed x51, local copies, waits for them, and re-layouts  15.5 us
    gather x4, local copies, waits for them, and re-layouts, on_device(): jnp.take(sources, sending, axis=0, mode='clip')  14.5 us
  transfers between devices with their start and end apart: 8, of which 6 were waited for; matrix products, arithmetic and copies ran while one was open for 13% of the time, Pallas kernels for 42%

profile of v4, /device:TPU:0, one launch (start us, length us, event | category | flops | bytes accessed | tf_op | source)
XLA Modules:
  0.0 544.4 jit_solution(2445111227937447329)
XLA Ops:
  6.5 3.2 slice.121
  11.5 23.1 %all-gather.4 = s32[16,1,204]{2,1,0:T(1,128)S(1)} all-gather(s32[1,1,204]{2,1,0:T(1,128)S(1)} %add_bitcast_fusion), channel_id=1, replica_groups=mesh['blk'=16,'ffn'=2] {'blk'}, dimensions={0}, use_global_device_ids=true | all-gather | bytes 13872 | tf_op jit(solution)/shard_map/all_gather | solution.py:416
  36.8 38.7 %shard_map.111 = (s32[4816]{0:T(1024)}, s32[16]{0:T(128)}, s32[16]{0:T(128)}, s32[301]{0:T(512)S(1)}, s32[76]{0:T(128)}) custom-call(s32[1616]{0:T(1024)} %reshape.137.index_ref, s32[1616]{0:T(1024)} %reshape.151.own_ref, s32[16]{0:T(128)} %get-tuple-element.285.count_ref, s32[16]{0:T(128)} %get-tuple-element.284.left_ref, s32[1]{0:T(128)} %bitcast.11.at_ref), custom_call_target="tpu_custom_call" | custom-call | bytes 25856 | tf_op jit(solution)/shard_map/pallas_call | solution.py:367
  78.7 2.5 pad_maximum_fusion.1
  81.2 4.3 gather_fusion.1
  85.9 2.5 constant_dynamic-update-slice_fusion.5
  91.5 4.7 pad_maximum_fusion
  96.2 3.4 gather_fusion.2
  99.8 3.6 gather_fusion.3
  103.5 3.3 gather_fusion.4
  107.3 2.7 constant_dynamic-update-slice_fusion.3
  110.0 11.2 %collective-permute-done.2 = bf16[13,128,128]{2,1,0:T(8,128)(2,1)S(1)} collective-permute-done((bf16[13,128,128]{2,1,0:T(8,128)(2,1)S(1)}, bf16[13,128,128]{2,1,0:T(8,128)(2,1)S(1)}, u32[]{:S(2)}, u32[]{:S(2)}) %collective-permute-start.2) | collective-permute-done | bytes 426016 | tf_op jit(solution)/shard_map/ppermute | solution.py:437
  122.1 4.3 collective-permute-done.3
  127.1 2.5 collective-permute-done.4
  130.3 5.7 %gather_fusion.5 = bf16[76,128,128]{2,1,0:T(8,128)(2,1)} fusion(bf16[214,128,128]{2,1,0:T(8,128)(2,1)} %constant_dynamic-update-slice_fusion, s32[1024]{0:T(1024)S(1)} %pad_clamp_fusion.2), kind=kCustom, calls=%fused_computation.5 | custom fusion | bytes 4981040 | tf_op jit(solution)/shard_map/jit(_take)/gather | solution.py:447
  136.2 4.8 gather_fusion.6
  144.3 5.5 %pmax.7 = s32[3]{0:T(128)S(1)} all-reduce(s32[3]{0:T(128)S(1)} %pad_add_fusion), channel_id=1, replica_groups=mesh['blk'=16,'ffn'=2] {'ffn'}, use_global_device_ids=true, to_apply=%region_4.5 | all-reduce | flops 3 | bytes 24 | tf_op jit(solution)/shard_map/pmax | solution.py:450
  155.0 2.8 copy.18
  159.2 3.5 fusion.7
  162.7 3.0 copy.19
  168.1 18.8 %shard_map.114 = (s32[2240]{0:T(1024)}, s32[4]{0:T(128)}) custom-call(s32[592]{0:T(1024)} %reshape_reshape.14.row_ref, s32[592]{0:T(1024)} %compare_select_fusion.1.col_ref), custom_call_target="tpu_custom_call" | custom-call | bytes 9472 | tf_op jit(solution)/shard_map/pallas_call | solution.py:61
  187.5 28.8 %shard_map.115 = (s32[3360]{0:T(1024)}, s32[4]{0:T(128)}) custom-call(s32[1024]{0:T(1024)} %reshape_reshape.15.row_ref, s32[1024]{0:T(1024)} %compare_select_fusion.col_ref), custom_call_target="tpu_custom_call" | custom-call | bytes 16384 | tf_op jit(solution)/shard_map/pallas_call | solution.py:61
  216.4 30.1 %shard_map.113 = (s32[3312]{0:T(1024)}, s32[2]{0:T(128)}) custom-call(s32[1216]{0:T(1024)} %reshape_reshape.13.row_ref, s32[1216]{0:T(1024)} %select_n.161.col_ref), custom_call_target="tpu_custom_call" | custom-call | bytes 19456 | tf_op jit(solution)/shard_map/pallas_call | solution.py:61
  246.5 43.1 %shard_map.116.sum_ref = f32[72,256,128]{2,1,0:T(8,128)} custom-call(s32[3360]{0:T(1024)} %get-tuple-element.274.field_ref, s32[4]{0:T(128)} %get-tuple-element.275.count_ref, s32[1]{0:T(128)} %bitcast.15.at_ref, bf16[37,256,128]{2,1,0:T(8,128)(2,1)} %pad.4.x_ref, bf16[16,64,128,128]{3,2,1,0:T(8,128)(2,1)} %bitcast.61, f32[72,1,128]{2,1,0:T(1,128)} %bitcast.63), custom_call_target="tpu_custom_call" | custom-call | flops 17179869184 | bytes 33554432 | tf_op jit(solution)/shard_map/pallas_call | solution.py:211
  289.6 103.1 %all-gather.12.cloned.1.call-done = bf16[1216,128,128]{2,1,0:T(8,128)(2,1)} async-done(((bf16[76,128,128]{2,1,0:T(8,128)(2,1)}), bf16[1216,128,128]{2,1,0:T(8,128)(2,1)}) %all-gather.12.cloned.1.call-update) | async-done | bytes 39845904 | tf_op jit(solution)/shard_map/all_gather | solution.py:412
  392.7 18.8 %shard_map.117.x_ref = bf16[73,256,128]{2,1,0:T(8,128)(2,1)S(1)} custom-call(s32[2240]{0:T(1024)} %get-tuple-element.269.field_ref, s32[4]{0:T(128)} %get-tuple-element.270.count_ref, s32[1]{0:T(128)} %bitcast.15.at_ref, bf16[37,256,128]{2,1,0:T(8,128)(2,1)} %pad.4.x_ref, bf16[16,76,128,128]{3,2,1,0:T(8,128)(2,1)} %bitcast.42, ...), custom_call_target="tpu_custom_call" | custom-call | flops 9932111872 | bytes 19398656 | tf_op jit(solution)/shard_map/pallas_call | solution.py:211
  411.5 38.2 %shard_map.118 = (f32[36,256,128]{2,1,0:T(8,128)}, bf16[256,4608]{1,0:T(8,128)(2,1)}) custom-call(s32[3312]{0:T(1024)} %get-tuple-element.267.field_ref, s32[2]{0:T(128)} %get-tuple-element.268.count_ref, s32[1]{0:T(128)} %bitcast.15.at_ref, bf16[73,256,128]{2,1,0:T(8,128)(2,1)S(1)} %shard_map.117.x_ref, bf16[16,76,128,128]{3,2,1,0:T(8,128)(2,1)} %bitcast.43), custom_call_target="tpu_custom_call" | custom-call | flops 20401094656 | bytes 39845888 | tf_op jit(solution)/shard_map/pallas_call | solution.py:211
  456.0 13.2 %shard_map.112 = (s32[1440]{0:T(1024)}, s32[2]{0:T(128)}) custom-call(s32[512]{0:T(512)} %reshape_reshape.12.row_ref, s32[512]{0:T(512)} %select_n.157.col_ref), custom_call_target="tpu_custom_call" | custom-call | bytes 8192 | tf_op jit(solution)/shard_map/pallas_call | solution.py:61
  469.3 10.0 %collective-permute-done.5 = bf16[256,2304]{1,0:T(8,128)(2,1)S(1)} collective-permute-done((bf16[256,2304]{1,0:T(8,128)(2,1)S(1)}, bf16[256,2304]{1,0:T(8,128)(2,1)S(1)}, u32[]{:S(2)}, u32[]{:S(2)}) %collective-permute-start.5) | collective-permute-done | bytes 1179680 | tf_op jit(solution)/shard_map/ppermute | solution.py:517
  479.4 42.3 %all-gather.16.cloned.1.call-done = bf16[512,128,128]{2,1,0:T(8,128)(2,1)} async-done(((bf16[32,128,128]{2,1,0:T(8,128)(2,1)}), bf16[512,128,128]{2,1,0:T(8,128)(2,1)}) %all-gather.16.cloned.1.call-update) | async-done | bytes 16777232 | tf_op jit(solution)/shard_map/all_gather | solution.py:412
  521.8 15.1 %conditional.1 = (bf16[256,2304]{1,0:T(8,128)(2,1)S(1)}) conditional(s32[]{:T(128)} %convert_element_type.29, (s32[]{:T(128)}, s32[1440]{0:T(1024)}, s32[2]{0:T(128)}, bf16[73,256,128]{2,1,0:T(8,128)(2,1)}, bf16[16,32,128,128]{3,2,1,0:T(8,128)(2,1)}, /*index=5*/f32[36,256,128]{2,1,0:T(8,128)}, bf16[256,4608]{1,0:T(8,128)(2,1)}, ...), branch_computations={%region_6.7_spmd, %region_7.10_spmd} | conditional | flops 15303196672 | bytes 87497360 | solution.py:591
  521.8 15.1 %branch_0_fun.1 = bf16[256,2304]{1,0:T(8,128)(2,1)S(1)} custom-call(s32[1440]{0:T(1024)} %get-tuple-element.197.field_ref, s32[2]{0:T(128)} %get-tuple-element.198.count_ref, s32[1]{0:T(128)} %bitcast.at_ref, bf16[73,256,128]{2,1,0:T(8,128)(2,1)} %get-tuple-element.200.x_ref, bf16[16,32,128,128]{3,2,1,0:T(8,128)(2,1)} %get-tuple-element.201.w_ref, ...), custom_call_target="tpu_custom_call" | custom-call | flops 8589934592 | bytes 16777216 | tf_op jit(solution)/shard_map/cond/branch_0_fun/pallas_call | solution.py:211
  (127 shorter events, 30.7 us)
Async XLA Ops:
  6.5 4.8 copy-start.19
  6.5 4.8 copy-start.20
  6.5 240.0 %all-gather.14.cloned.1.call-start = ((), (), s32[]{:S(2)}) async-start(), calls=%async_computation.1 | async-start | bytes 35651584 | tf_op jit(solution)/shard_map/all_gather | solution.py:412
  9.7 69.0 %copy-start.1 = (bf16[1,1,101,128,128]{4,3,2,1,0:T(8,128)(2,1)S(1)}, bf16[1,1,101,128,128]{4,3,2,1,0:T(8,128)(2,1)}, u32[]{:S(2)}) copy-start(bf16[1,1,101,128,128]{4,3,2,1,0:T(8,128)(2,1)} %param.22) | copy-start | bytes 9928708
  9.7 382.9 %all-gather.12.cloned.1.call-start = ((), (), s32[]{:S(2)}) async-start(), calls=%async_computation | async-start | bytes 42336256 | tf_op jit(solution)/shard_map/all_gather | solution.py:412
  75.6 60.5 %copy-start.21 = (s32[301]{0:T(512)}, s32[301]{0:T(512)S(1)}, u32[]{:S(2)}) copy-start(s32[301]{0:T(512)S(1)} %get-tuple-element.273) | copy-start | bytes 3616
  77.6 1.1 copy-start.2
  78.7 7.0 %copy-start.18 = (s32[76]{0:T(128)S(1)}, s32[76]{0:T(128)}, u32[]{:S(2)}) copy-start(s32[76]{0:T(128)} %get-tuple-element.272) | copy-start | bytes 916
  85.5 4.9 collective-permute-start.1
  88.5 3.1 copy-start.3
  90.4 1.2 copy-start.4
  99.7 21.6 %collective-permute-start.2 = (bf16[13,128,128]{2,1,0:T(8,128)(2,1)S(1)}, bf16[13,128,128]{2,1,0:T(8,128)(2,1)S(1)}, u32[]{:S(2)}, u32[]{:S(2)}) collective-permute-start(bf16[13,128,128]{2,1,0:T(8,128)(2,1)S(1)} %gather_fusion.2), channel_id=1, source_target_pairs={{0,4},{2,6},{4,0},{6,2},{8,12},{10,14},{12,8},{14,10},{16,20},{18,... | collective-permute-start | bytes 1277960 | tf_op jit(solution)/shard_map/ppermute | solution.py:437
  103.4 23.0 %collective-permute-start.3 = (bf16[10,128,128]{2,1,0:T(8,128)(2,1)S(1)}, bf16[10,128,128]{2,1,0:T(8,128)(2,1)S(1)}, u32[]{:S(2)}, u32[]{:S(2)}) collective-permute-start(bf16[10,128,128]{2,1,0:T(8,128)(2,1)S(1)} %gather_fusion.3), channel_id=1, source_target_pairs={{0,8},{2,10},{4,12},{6,14},{8,0},{10,2},{12,4},{14,6},{16,24},{18,... | collective-permute-start | bytes 983048 | tf_op jit(solution)/shard_map/ppermute | solution.py:437
  106.8 22.8 %collective-permute-start.4 = (bf16[8,128,128]{2,1,0:T(8,128)(2,1)S(1)}, bf16[8,128,128]{2,1,0:T(8,128)(2,1)S(1)}, u32[]{:S(2)}, u32[]{:S(2)}) collective-permute-start(bf16[8,128,128]{2,1,0:T(8,128)(2,1)S(1)} %gather_fusion.4), channel_id=1, source_target_pairs={{0,16},{2,18},{4,20},{6,22},{8,24},{10,26},{12,28},{14,30},{16,0},... | collective-permute-start | bytes 786440 | tf_op jit(solution)/shard_map/ppermute | solution.py:437
  136.0 5.0 copy-start.17
  136.0 5.6 %copy-start.16 = (s32[16]{0:T(128)S(1)}, s32[16]{0:T(128)}, u32[]{:S(2)}) copy-start(s32[16]{0:T(128)} %get-tuple-element.261) | copy-start | bytes 196
  136.0 14.5 %copy-start.9 = (s32[4816]{0:T(1024)S(1)}, s32[4816]{0:T(1024)}, u32[]{:S(2)}) copy-start(s32[4816]{0:T(1024)} %get-tuple-element.264) | copy-start | bytes 57796
  136.0 16.3 %copy-start.13 = (s32[16]{0:T(128)S(1)}, s32[16]{0:T(128)}, u32[]{:S(2)}) copy-start(s32[16]{0:T(128)} %get-tuple-element.284.left_ref) | copy-start | bytes 196
  136.1 385.7 %all-gather.16.cloned.1.call-start = ((), (), s32[]{:S(2)}) async-start(), calls=%async_computation.2 | async-start | bytes 17825792 | tf_op jit(solution)/shard_map/all_gather | solution.py:412
  149.8 305.1 %copy-start.14 = (s32[3]{0:T(128)}, s32[3]{0:T(128)S(1)}, u32[]{:S(2)}) copy-start(s32[3]{0:T(128)S(1)} %pmax.7) | copy-start | bytes 40
  150.6 3.7 copy-start.6
  153.0 0.6 copy-start.8
  157.9 1.3 copy-start.10
  157.9 1.3 copy-start.11
  411.5 38.2 %copy-start = (bf16[73,256,128]{2,1,0:T(8,128)(2,1)}, bf16[73,256,128]{2,1,0:T(8,128)(2,1)S(1)}, u32[]{:S(2)}) copy-start(bf16[73,256,128]{2,1,0:T(8,128)(2,1)S(1)} %shard_map.117.x_ref) | copy-start | bytes 14352388
  411.5 41.1 %copy-start.12 = (f32[2304]{0:T(1024)S(1)}, f32[2304]{0:T(1024)}, u32[]{:S(2)}) copy-start(f32[2304]{0:T(1024)} %param.25) | copy-start | bytes 27652
  411.5 41.1 %copy-start.7 = (s32[16,301]{1,0:T(8,128)S(1)}, s32[16,301]{1,0:T(8,128)}, u32[]{:S(2)}) copy-start(s32[16,301]{1,0:T(8,128)} %copy-done.6) | copy-start | bytes 57796
  451.0 28.3 %collective-permute-start.5 = (bf16[256,2304]{1,0:T(8,128)(2,1)S(1)}, bf16[256,2304]{1,0:T(8,128)(2,1)S(1)}, u32[]{:S(2)}, u32[]{:S(2)}) collective-permute-start(bf16[256,2304]{1,0:T(8,128)(2,1)S(1)} %constant_dynamic-slice_fusion.1), channel_id=1, source_target_pairs={{0,1},{1,0},{2,3},{3,2},{4,5},{5,4},{6,7},{7,6},{8,9},{9,8},{10,11... | collective-permute-start | bytes 3538952 | tf_op jit(solution)/shard_map/ppermute | solution.py:517
  536.9 1.0 copy-start.5
Sparse Core Ops, SparseCore 0:
  9.9 183.4 all-gather.13
  194.9 197.7 all-gather.11
  394.9 126.8 all-gather.15

commit v5 on v3

--- a/solution.py
+++ b/solution.py
@@ -89,7 +89,17 @@
             one(turn * UNROLL + u)
         return carry
 
-    lax.fori_loop(0, lax.div(count_ref[step] + UNROLL - 1, jnp.int32(UNROLL)), several, 0)
+    whole = lax.div(count_ref[step], jnp.int32(UNROLL))
+    done = whole * UNROLL
+
+    def few(turn, carry):
+        for u in range(UNROLL // 2):
+            one(done + turn * (UNROLL // 2) + u)
+        return carry
+
+    left_over = count_ref[step] - done + UNROLL // 2 - 1
+    lax.fori_loop(0, whole, several, 0)
+    lax.fori_loop(0, lax.div(left_over, jnp.int32(UNROLL // 2)), few, 0)
 
 
 def for_blocks(count, work):
@@ -169,22 +179,28 @@
     x_ref, w_ref, sum_ref, token_ref, other_ref, bias_ref, out_ref, acc,
 ):
     blocks, width = acc.shape[0], acc.shape[2]
+    part = token_ref.shape[0]
+    rows = pl.ds(pl.multiple_of(pl.program_id(0) * part, part), part)
 
     @at_start
     def _():
         def fill(c):
-            acc[c] = sum_ref[c]
+            acc[c] = jnp.zeros(acc.shape[1:], acc.dtype)
 
         for_blocks(blocks, fill)
 
+    def add_rows(c):
+        cols = columns(c, width)
+        value = token_ref[:, cols].astype(jnp.float32) + (sum_ref[c] + other_ref[:, cols])
+        acc[c, rows] += value + bias_ref[:, cols]
+
+    for_blocks(blocks, add_rows)
     add_block(field_ref, count_ref, x_ref, w_ref, acc, group)
 
     @at_end
     def _():
         def finish(c):
-            cols = columns(c, width)
-            value = token_ref[:, cols].astype(jnp.float32) + (acc[c] + other_ref[:, cols])
-            out_ref[:, cols] = (value + bias_ref[:, cols]).astype(out_ref.dtype)
+            out_ref[:, columns(c, width)] = acc[c].astype(out_ref.dtype)
 
         for_blocks(blocks, finish)
 
@@ -551,7 +567,9 @@
 
     share_blocks = share // side
     last_rows, last_cols = last_codes // second_blocks, last_codes % second_blocks % share_blocks
-    last_plan = planned(last_rows, last_cols, last_own, share_blocks, first_blocks, 4, 4)
+    last_steps = 4 if shards % 4 == 0 and token_rows % 64 == 0 else 1
+    last_part = token_rows // last_steps
+    last_plan = planned(last_rows, last_cols, last_own, share_blocks, first_blocks, last_steps, 4)
     bias_row = fc2_bias.reshape(1, share)
     last_plan, branch, bias_row = lax.optimization_barrier((last_plan, branch, bias_row))
     last_pass = functools.partial(
@@ -564,22 +582,14 @@
         hidden,
         tiles2b,
         more_specs=[
-            pl.BlockSpec(
-                (share_blocks, token_rows, side),
-                lambda i, fields, counts, at: (at[0], 0, 0),
-                pipeline_mode=pl.Buffered(1),
-            ),
-            pl.BlockSpec(
-                (token_rows, share),
-                lambda i, fields, counts, at: (0, at[0]),
-                pipeline_mode=pl.Buffered(1),
-            ),
-            fixed((token_rows, share)),
+            pl.BlockSpec((share_blocks, last_part, side), lambda i, fields, counts, at: (at[0], i, 0)),
+            pl.BlockSpec((last_part, share), lambda i, fields, counts, at: (i, at[0])),
+            pl.BlockSpec((last_part, share), lambda i, *_: (i, 0)),
             fixed((1, share)),
         ],
         out_shapes=[jax.ShapeDtypeStruct((token_rows, share), jnp.bfloat16)],
         blocks=share_blocks,
-        steps=4,
+        steps=last_steps,
         group=4,
         vmem=LAST_VMEM_BYTES,
         plan=last_plan,

time: 511 us -> 509 us (level)
  transfers between devices with their start and end apart: 8 -> 8, of which waited for: 6 -> 6; matrix products, arithmetic and copies ran while one was open for 14% -> 14% of each run, Pallas kernels for 46% -> 45%
where the time goes in v5:
time: 509 us
  Pallas kernels  248 us (49%)
  waiting for transfers between devices  137 us (27%)
  local copies, waits for them, and re-layouts  58.5 us (11%)
  blocking collectives  28 us (6%)
  other arithmetic  17.8 us (3%)
  between operations  17 us (3%)
    pallas_call x4, Pallas kernels, tile_pass(): pl.pallas_call(functools.partial(kernel, group), out_shape=out_shapes, gr...  117 us
    all_gather x3, waiting for transfers between devices, gathered(): lax.all_gather(value, 'blk', axis=0, tiled=True)  109 us
    pallas_call x4, Pallas kernels, group_up(): pl.pallas_call(functools.partial(group_kernel, group, size, zero_row), ou...  91.9 us
    pallas_call x1, Pallas kernels, laid_out(): pl.pallas_call(functools.partial(layout_kernel, levels, capacity), out_sh...  39.8 us
    all_gather x1, blocking collectives, on_device(): meta = lax.all_gather(meta, 'blk', axis=0, tiled=True)  23.1 us
    ppermute x4, waiting for transfers between devices, on_device(): lax.ppermute(jnp.take(sources, sending, axis=0, mode='clip'), 'blk', [(i,...  18.3 us
    unnamed x49, local copies, waits for them, and re-layouts  14.9 us
    gather x4, local copies, waits for them, and re-layouts, on_device(): jnp.take(sources, sending, axis=0, mode='clip')  14.4 us
  transfers between devices with their start and end apart: 8, of which 6 were waited for; matrix products, arithmetic and copies ran while one was open for 14% of the time, Pallas kernels for 45%

profile of v5, /device:TPU:0, one launch (start us, length us, event | category | flops | bytes accessed | tf_op | source)
XLA Modules:
  0.0 509.0 jit_solution(7348237307711692286)
XLA Ops:
  6.5 3.2 slice.121
  11.5 23.1 %all-gather.4 = s32[16,1,204]{2,1,0:T(1,128)S(1)} all-gather(s32[1,1,204]{2,1,0:T(1,128)S(1)} %add_bitcast_fusion), channel_id=1, replica_groups=mesh['blk'=16,'ffn'=2] {'blk'}, dimensions={0}, use_global_device_ids=true | all-gather | bytes 13872 | tf_op jit(solution)/shard_map/all_gather | solution.py:432
  36.8 39.8 %shard_map.111 = (s32[4816]{0:T(1024)}, s32[16]{0:T(128)}, s32[16]{0:T(128)}, s32[301]{0:T(512)S(1)}, s32[76]{0:T(128)}) custom-call(s32[1616]{0:T(1024)} %reshape.137.index_ref, s32[1616]{0:T(1024)} %reshape.151.own_ref, s32[16]{0:T(128)} %get-tuple-element.285.count_ref, s32[16]{0:T(128)} %get-tuple-element.284.left_ref, s32[1]{0:T(128)} %bitcast.11.at_ref), custom_call_target="tpu_custom_call" | custom-call | bytes 25856 | tf_op jit(solution)/shard_map/pallas_call | solution.py:383
  79.8 2.5 pad_maximum_fusion.1
  82.2 4.3 gather_fusion.1
  87.4 2.5 constant_dynamic-update-slice_fusion.5
  93.0 4.6 pad_maximum_fusion
  97.6 3.3 gather_fusion.2
  101.1 3.4 gather_fusion.3
  104.6 3.4 gather_fusion.4
  108.1 2.8 constant_dynamic-update-slice_fusion.3
  110.9 11.6 %collective-permute-done.2 = bf16[13,128,128]{2,1,0:T(8,128)(2,1)S(1)} collective-permute-done((bf16[13,128,128]{2,1,0:T(8,128)(2,1)S(1)}, bf16[13,128,128]{2,1,0:T(8,128)(2,1)S(1)}, u32[]{:S(2)}, u32[]{:S(2)}) %collective-permute-start.2) | collective-permute-done | bytes 426016 | tf_op jit(solution)/shard_map/ppermute | solution.py:453
  123.3 4.2 collective-permute-done.3
  128.2 2.5 collective-permute-done.4
  131.4 5.6 %gather_fusion.5 = bf16[75,128,128]{2,1,0:T(8,128)(2,1)} fusion(bf16[214,128,128]{2,1,0:T(8,128)(2,1)} %constant_dynamic-update-slice_fusion, s32[1024]{0:T(1024)S(1)} %pad_clamp_fusion.2), kind=kCustom, calls=%fused_computation.5 | custom fusion | bytes 4915500 | tf_op jit(solution)/shard_map/jit(_take)/gather | solution.py:463
  137.2 4.8 gather_fusion.6
  145.3 4.8 pmax.7
  154.2 2.8 copy.18
  158.4 3.5 fusion.7
  161.9 3.0 copy.19
  167.2 18.8 %shard_map.114 = (s32[2240]{0:T(1024)}, s32[4]{0:T(128)}) custom-call(s32[592]{0:T(1024)} %reshape_reshape.14.row_ref, s32[592]{0:T(1024)} %compare_select_fusion.1.col_ref), custom_call_target="tpu_custom_call" | custom-call | bytes 9472 | tf_op jit(solution)/shard_map/pallas_call | solution.py:61
  186.7 28.8 %shard_map.115 = (s32[3360]{0:T(1024)}, s32[4]{0:T(128)}) custom-call(s32[1024]{0:T(1024)} %reshape_reshape.15.row_ref, s32[1024]{0:T(1024)} %compare_select_fusion.col_ref), custom_call_target="tpu_custom_call" | custom-call | bytes 16384 | tf_op jit(solution)/shard_map/pallas_call | solution.py:61
  215.5 29.8 %shard_map.113 = (s32[3312]{0:T(1024)}, s32[2]{0:T(128)}) custom-call(s32[1200]{0:T(1024)} %reshape_reshape.13.row_ref, s32[1200]{0:T(1024)} %select_n.161.col_ref), custom_call_target="tpu_custom_call" | custom-call | bytes 19200 | tf_op jit(solution)/shard_map/pallas_call | solution.py:61
  245.3 42.8 %shard_map.116.sum_ref = f32[72,256,128]{2,1,0:T(8,128)} custom-call(s32[3360]{0:T(1024)} %get-tuple-element.274.field_ref, s32[4]{0:T(128)} %get-tuple-element.275.count_ref, s32[1]{0:T(128)} %bitcast.15.at_ref, bf16[37,256,128]{2,1,0:T(8,128)(2,1)} %pad.4.x_ref, bf16[16,64,128,128]{3,2,1,0:T(8,128)(2,1)} %bitcast.59, f32[72,1,128]{2,1,0:T(1,128)} %bitcast.63), custom_call_target="tpu_custom_call" | custom-call | flops 17179869184 | bytes 33554432 | tf_op jit(solution)/shard_map/pallas_call | solution.py:227
  288.1 102.1 %all-gather.12.cloned.1.call-done = bf16[1200,128,128]{2,1,0:T(8,128)(2,1)} async-done(((bf16[75,128,128]{2,1,0:T(8,128)(2,1)}), bf16[1200,128,128]{2,1,0:T(8,128)(2,1)}) %all-gather.12.cloned.1.call-update) | async-done | bytes 39321616 | tf_op jit(solution)/shard_map/all_gather | solution.py:428
  390.2 20.7 %shard_map.117.x_ref = bf16[73,256,128]{2,1,0:T(8,128)(2,1)S(1)} custom-call(s32[2240]{0:T(1024)} %get-tuple-element.269.field_ref, s32[4]{0:T(128)} %get-tuple-element.270.count_ref, s32[1]{0:T(128)} %bitcast.15.at_ref, bf16[37,256,128]{2,1,0:T(8,128)(2,1)} %pad.4.x_ref, bf16[16,75,128,128]{3,2,1,0:T(8,128)(2,1)} %bitcast.40, ...), custom_call_target="tpu_custom_call" | custom-call | flops 9932111872 | bytes 19398656 | tf_op jit(solution)/shard_map/pallas_call | solution.py:227
  411.0 35.2 %shard_map.118 = (f32[36,256,128]{2,1,0:T(8,128)}, bf16[256,4608]{1,0:T(8,128)(2,1)}) custom-call(s32[3312]{0:T(1024)} %get-tuple-element.267.field_ref, s32[2]{0:T(128)} %get-tuple-element.268.count_ref, s32[1]{0:T(128)} %bitcast.15.at_ref, bf16[73,256,128]{2,1,0:T(8,128)(2,1)S(1)} %shard_map.117.x_ref, bf16[16,75,128,128]{3,2,1,0:T(8,128)(2,1)} %bitcast.41), custom_call_target="tpu_custom_call" | custom-call | flops 20132659200 | bytes 39321600 | tf_op jit(solution)/shard_map/pallas_call | solution.py:227
  452.5 14.5 %shard_map.112 = (s32[1728]{0:T(1024)}, s32[4]{0:T(128)}) custom-call(s32[528]{0:T(1024)} %reshape_reshape.12.row_ref, s32[528]{0:T(1024)} %select_n.157.col_ref), custom_call_target="tpu_custom_call" | custom-call | bytes 8448 | tf_op jit(solution)/shard_map/pallas_call | solution.py:61
  467.0 9.0 %collective-permute-done.5 = bf16[256,2304]{1,0:T(8,128)(2,1)S(1)} collective-permute-done((bf16[256,2304]{1,0:T(8,128)(2,1)S(1)}, bf16[256,2304]{1,0:T(8,128)(2,1)S(1)}, u32[]{:S(2)}, u32[]{:S(2)}) %collective-permute-start.5) | collective-permute-done | bytes 1179680 | tf_op jit(solution)/shard_map/ppermute | solution.py:533
  476.1 7.3 %all-gather.16.cloned.1.call-done = bf16[528,128,128]{2,1,0:T(8,128)(2,1)} async-done(((bf16[33,128,128]{2,1,0:T(8,128)(2,1)}), bf16[528,128,128]{2,1,0:T(8,128)(2,1)}) %all-gather.16.cloned.1.call-update) | async-done | bytes 17301520 | tf_op jit(solution)/shard_map/all_gather | solution.py:428
  483.4 18.1 %conditional.1 = (bf16[256,2304]{1,0:T(8,128)(2,1)S(1)}) conditional(s32[]{:T(128)} %convert_element_type.29, (s32[]{:T(128)}, s32[1728]{0:T(1024)}, s32[4]{0:T(128)}, bf16[73,256,128]{2,1,0:T(8,128)(2,1)}, bf16[16,33,128,128]{3,2,1,0:T(8,128)(2,1)}, /*index=5*/f32[36,256,128]{2,1,0:T(8,128)}, bf16[256,4608]{1,0:T(8,128)(2,1)}, ...), branch_computations={%region_6.7_spmd, %region_7.10_spmd} | conditional | flops 15571632128 | bytes 88068552 | solution.py:601
  483.4 18.1 %branch_0_fun.1 = bf16[256,2304]{1,0:T(8,128)(2,1)S(1)} custom-call(s32[1728]{0:T(1024)} %get-tuple-element.197.field_ref, s32[4]{0:T(128)} %get-tuple-element.198.count_ref, s32[1]{0:T(128)} %bitcast.at_ref, bf16[73,256,128]{2,1,0:T(8,128)(2,1)} %get-tuple-element.200.x_ref, bf16[16,33,128,128]{3,2,1,0:T(8,128)(2,1)} %get-tuple-element.201.w_ref, ...), custom_call_target="tpu_custom_call" | custom-call | flops 8858370048 | bytes 17301504 | tf_op jit(solution)/shard_map/cond/branch_0_fun/pallas_call | solution.py:227
  (125 shorter events, 29.4 us)
Async XLA Ops:
  6.5 4.8 copy-start.17
  6.5 4.8 copy-start.18
  6.5 238.8 %all-gather.14.cloned.1.call-start = ((), (), s32[]{:S(2)}) async-start(), calls=%async_computation.1 | async-start | bytes 35651584 | tf_op jit(solution)/shard_map/all_gather | solution.py:428
  9.7 70.1 %copy-start = (bf16[1,1,101,128,128]{4,3,2,1,0:T(8,128)(2,1)S(1)}, bf16[1,1,101,128,128]{4,3,2,1,0:T(8,128)(2,1)}, u32[]{:S(2)}) copy-start(bf16[1,1,101,128,128]{4,3,2,1,0:T(8,128)(2,1)} %param.22) | copy-start | bytes 9928708
  9.7 380.5 %all-gather.12.cloned.1.call-start = ((), (), s32[]{:S(2)}) async-start(), calls=%async_computation | async-start | bytes 41779200 | tf_op jit(solution)/shard_map/all_gather | solution.py:428
  76.6 60.5 %copy-start.20 = (s32[301]{0:T(512)}, s32[301]{0:T(512)S(1)}, u32[]{:S(2)}) copy-start(s32[301]{0:T(512)S(1)} %get-tuple-element.273) | copy-start | bytes 3616
  78.6 1.1 copy-start.1
  79.8 7.5 %copy-start.16 = (s32[76]{0:T(128)S(1)}, s32[76]{0:T(128)}, u32[]{:S(2)}) copy-start(s32[76]{0:T(128)} %get-tuple-element.272) | copy-start | bytes 916
  86.5 5.3 %collective-permute-start.1 = (bf16[45,128,128]{2,1,0:T(8,128)(2,1)}, bf16[45,128,128]{2,1,0:T(8,128)(2,1)S(1)}, u32[]{:S(2)}, u32[]{:S(2)}) collective-permute-start(bf16[45,128,128]{2,1,0:T(8,128)(2,1)} %gather_fusion.1), channel_id=1, source_target_pairs={{0,2},{2,0},{4,6},{6,4},{8,10},{10,8},{12,14},{14,12},{16,18},{18,... | collective-permute-start | bytes 4423688 | tf_op jit(solution)/shard_map/ppermute | solution.py:453
  89.9 3.1 copy-start.2
  91.8 1.2 copy-start.3
  100.9 21.5 %collective-permute-start.2 = (bf16[13,128,128]{2,1,0:T(8,128)(2,1)S(1)}, bf16[13,128,128]{2,1,0:T(8,128)(2,1)S(1)}, u32[]{:S(2)}, u32[]{:S(2)}) collective-permute-start(bf16[13,128,128]{2,1,0:T(8,128)(2,1)S(1)} %gather_fusion.2), channel_id=1, source_target_pairs={{0,4},{2,6},{4,0},{6,2},{8,12},{10,14},{12,8},{14,10},{16,20},{18,... | collective-permute-start | bytes 1277960 | tf_op jit(solution)/shard_map/ppermute | solution.py:453
  104.5 22.9 %collective-permute-start.3 = (bf16[10,128,128]{2,1,0:T(8,128)(2,1)S(1)}, bf16[10,128,128]{2,1,0:T(8,128)(2,1)S(1)}, u32[]{:S(2)}, u32[]{:S(2)}) collective-permute-start(bf16[10,128,128]{2,1,0:T(8,128)(2,1)S(1)} %gather_fusion.3), channel_id=1, source_target_pairs={{0,8},{2,10},{4,12},{6,14},{8,0},{10,2},{12,4},{14,6},{16,24},{18,... | collective-permute-start | bytes 983048 | tf_op jit(solution)/shard_map/ppermute | solution.py:453
  108.0 22.7 %collective-permute-start.4 = (bf16[8,128,128]{2,1,0:T(8,128)(2,1)S(1)}, bf16[8,128,128]{2,1,0:T(8,128)(2,1)S(1)}, u32[]{:S(2)}, u32[]{:S(2)}) collective-permute-start(bf16[8,128,128]{2,1,0:T(8,128)(2,1)S(1)} %gather_fusion.4), channel_id=1, source_target_pairs={{0,16},{2,18},{4,20},{6,22},{8,24},{10,26},{12,28},{14,30},{16,0},... | collective-permute-start | bytes 786440 | tf_op jit(solution)/shard_map/ppermute | solution.py:453
  137.0 5.0 copy-start.15
  137.0 5.7 %copy-start.14 = (s32[16]{0:T(128)S(1)}, s32[16]{0:T(128)}, u32[]{:S(2)}) copy-start(s32[16]{0:T(128)} %get-tuple-element.261) | copy-start | bytes 196
  137.0 13.9 %copy-start.8 = (s32[4816]{0:T(1024)S(1)}, s32[4816]{0:T(1024)}, u32[]{:S(2)}) copy-start(s32[4816]{0:T(1024)} %get-tuple-element.264) | copy-start | bytes 57796
  137.0 15.7 %copy-start.12 = (s32[16]{0:T(128)S(1)}, s32[16]{0:T(128)}, u32[]{:S(2)}) copy-start(s32[16]{0:T(128)} %get-tuple-element.284.left_ref) | copy-start | bytes 196
  137.0 346.4 %all-gather.16.cloned.1.call-start = ((), (), s32[]{:S(2)}) async-start(), calls=%async_computation.2 | async-start | bytes 18382848 | tf_op jit(solution)/shard_map/all_gather | solution.py:428
  151.0 2.5 copy-start.5
  157.0 1.3 copy-start.9
  157.0 1.3 copy-start.10
  410.9 35.2 %copy-start.4 = (bf16[73,256,128]{2,1,0:T(8,128)(2,1)}, bf16[73,256,128]{2,1,0:T(8,128)(2,1)S(1)}, u32[]{:S(2)}) copy-start(bf16[73,256,128]{2,1,0:T(8,128)(2,1)S(1)} %shard_map.117.x_ref) | copy-start | bytes 14352388
  410.9 38.1 %copy-start.11 = (f32[2304]{0:T(1024)S(1)}, f32[2304]{0:T(1024)}, u32[]{:S(2)}) copy-start(f32[2304]{0:T(1024)} %param.25) | copy-start | bytes 27652
  410.9 38.7 %copy-start.6 = (s32[16,301]{1,0:T(8,128)S(1)}, s32[16,301]{1,0:T(8,128)}, u32[]{:S(2)}) copy-start(s32[16,301]{1,0:T(8,128)} %copy-done.5) | copy-start | bytes 57796
  410.9 40.3 %copy-start.13 = (s32[3]{0:T(128)S(1)}, s32[3]{0:T(128)}, u32[]{:S(2)}) copy-start(s32[3]{0:T(128)} %pmax.7) | copy-start | bytes 40
  447.5 28.4 %collective-permute-start.5 = (bf16[256,2304]{1,0:T(8,128)(2,1)S(1)}, bf16[256,2304]{1,0:T(8,128)(2,1)S(1)}, u32[]{:S(2)}, u32[]{:S(2)}) collective-permute-start(bf16[256,2304]{1,0:T(8,128)(2,1)S(1)} %constant_dynamic-slice_fusion.1), channel_id=1, source_target_pairs={{0,1},{1,0},{2,3},{3,2},{4,5},{5,4},{6,7},{7,6},{8,9},{9,8},{10,11... | collective-permute-start | bytes 3538952 | tf_op jit(solution)/shard_map/ppermute | solution.py:533
  501.5 1.0 copy-start.21
Sparse Core Ops, SparseCore 0:
  9.9 183.4 all-gather.13
  194.9 195.2 all-gather.11
  391.8 91.5 all-gather.15

commit v6 on v5

--- a/solution.py
+++ b/solution.py
@@ -569,7 +569,7 @@
     last_rows, last_cols = last_codes // second_blocks, last_codes % second_blocks % share_blocks
     last_steps = 4 if shards % 4 == 0 and token_rows % 64 == 0 else 1
     last_part = token_rows // last_steps
-    last_plan = planned(last_rows, last_cols, last_own, share_blocks, first_blocks, last_steps, 4)
+    last_plan = planned(last_rows, last_cols, last_own, share_blocks, first_blocks, last_steps, 3)
     bias_row = fc2_bias.reshape(1, share)
     last_plan, branch, bias_row = lax.optimization_barrier((last_plan, branch, bias_row))
     last_pass = functools.partial(
@@ -590,7 +590,7 @@
         out_shapes=[jax.ShapeDtypeStruct((token_rows, share), jnp.bfloat16)],
         blocks=share_blocks,
         steps=last_steps,
-        group=4,
+        group=3,
         vmem=LAST_VMEM_BYTES,
         plan=last_plan,
     )

time: 509 us -> 510 us (level)
  no operation moved by 1% of the time
where the time goes in v6:
time: 510 us; the launch traced here: 509 us
  Pallas kernels  248 us (49%)
  waiting for transfers between devices  136 us (27%)
  local copies, waits for them, and re-layouts  58.8 us (12%)
  blocking collectives  28 us (5%)
  other arithmetic  17.8 us (3%)
  between operations  16.9 us (3%)
    pallas_call x4, Pallas kernels, tile_pass(): pl.pallas_call(functools.partial(kernel, group), out_shape=out_shapes, gr...  116 us
    all_gather x3, waiting for transfers between devices, gathered(): lax.all_gather(value, 'blk', axis=0, tiled=True)  109 us
    pallas_call x4, Pallas kernels, group_up(): pl.pallas_call(functools.partial(group_kernel, group, size, zero_row), ou...  92 us
    pallas_call x1, Pallas kernels, laid_out(): pl.pallas_call(functools.partial(layout_kernel, levels, capacity), out_sh...  40.1 us
    all_gather x1, blocking collectives, on_device(): meta = lax.all_gather(meta, 'blk', axis=0, tiled=True)  23.1 us
    ppermute x4, waiting for transfers between devices, on_device(): lax.ppermute(jnp.take(sources, sending, axis=0, mode='clip'), 'blk', [(i,...  18.2 us
    unnamed x49, local copies, waits for them, and re-layouts  14.9 us
    gather x4, local copies, waits for them, and re-layouts, on_device(): jnp.take(sources, sending, axis=0, mode='clip')  14.6 us
  transfers between devices with their start and end apart: 8, of which 6 were waited for; matrix products, arithmetic and copies ran while one was open for 14% of the time, Pallas kernels for 45%

profile of v6, /device:TPU:0, one launch (start us, length us, event | category | flops | bytes accessed | tf_op | source)
XLA Modules:
  0.0 508.6 jit_solution(15669338192540218872)
XLA Ops:
  6.5 3.2 slice.121
  11.5 23.1 %all-gather.4 = s32[16,1,204]{2,1,0:T(1,128)S(1)} all-gather(s32[1,1,204]{2,1,0:T(1,128)S(1)} %add_bitcast_fusion), channel_id=1, replica_groups=mesh['blk'=16,'ffn'=2] {'blk'}, dimensions={0}, use_global_device_ids=true | all-gather | bytes 13872 | tf_op jit(solution)/shard_map/all_gather | solution.py:432
  36.8 40.1 %shard_map.111 = (s32[4816]{0:T(1024)}, s32[16]{0:T(128)}, s32[16]{0:T(128)}, s32[301]{0:T(512)S(1)}, s32[76]{0:T(128)}) custom-call(s32[1616]{0:T(1024)} %reshape.137.index_ref, s32[1616]{0:T(1024)} %reshape.151.own_ref, s32[16]{0:T(128)} %get-tuple-element.285.count_ref, s32[16]{0:T(128)} %get-tuple-element.284.left_ref, s32[1]{0:T(128)} %bitcast.11.at_ref), custom_call_target="tpu_custom_call" | custom-call | bytes 25856 | tf_op jit(solution)/shard_map/pallas_call | solution.py:383
  80.1 2.5 pad_maximum_fusion.1
  82.5 4.5 gather_fusion.1
  87.6 2.5 constant_dynamic-update-slice_fusion.5
  93.2 4.6 pad_maximum_fusion
  97.8 3.3 gather_fusion.2
  101.3 3.4 gather_fusion.3
  104.8 3.4 gather_fusion.4
  108.5 2.7 constant_dynamic-update-slice_fusion.3
  111.2 11.5 %collective-permute-done.2 = bf16[13,128,128]{2,1,0:T(8,128)(2,1)S(1)} collective-permute-done((bf16[13,128,128]{2,1,0:T(8,128)(2,1)S(1)}, bf16[13,128,128]{2,1,0:T(8,128)(2,1)S(1)}, u32[]{:S(2)}, u32[]{:S(2)}) %collective-permute-start.2) | collective-permute-done | bytes 426016 | tf_op jit(solution)/shard_map/ppermute | solution.py:453
  123.5 4.2 collective-permute-done.3
  128.4 2.5 collective-permute-done.4
  131.6 5.6 %gather_fusion.5 = bf16[75,128,128]{2,1,0:T(8,128)(2,1)} fusion(bf16[214,128,128]{2,1,0:T(8,128)(2,1)} %constant_dynamic-update-slice_fusion, s32[1024]{0:T(1024)S(1)} %pad_clamp_fusion.2), kind=kCustom, calls=%fused_computation.5 | custom fusion | bytes 4915500 | tf_op jit(solution)/shard_map/jit(_take)/gather | solution.py:463
  137.4 4.8 gather_fusion.6
  145.4 4.8 pmax.7
  154.4 2.8 copy.18
  158.6 3.5 fusion.7
  162.0 3.2 copy.19
  167.6 18.8 %shard_map.114 = (s32[2240]{0:T(1024)}, s32[4]{0:T(128)}) custom-call(s32[592]{0:T(1024)} %reshape_reshape.14.row_ref, s32[592]{0:T(1024)} %compare_select_fusion.1.col_ref), custom_call_target="tpu_custom_call" | custom-call | bytes 9472 | tf_op jit(solution)/shard_map/pallas_call | solution.py:61
  187.0 28.8 %shard_map.115 = (s32[3360]{0:T(1024)}, s32[4]{0:T(128)}) custom-call(s32[1024]{0:T(1024)} %reshape_reshape.15.row_ref, s32[1024]{0:T(1024)} %compare_select_fusion.col_ref), custom_call_target="tpu_custom_call" | custom-call | bytes 16384 | tf_op jit(solution)/shard_map/pallas_call | solution.py:61
  215.8 29.8 %shard_map.113 = (s32[3312]{0:T(1024)}, s32[2]{0:T(128)}) custom-call(s32[1200]{0:T(1024)} %reshape_reshape.13.row_ref, s32[1200]{0:T(1024)} %select_n.161.col_ref), custom_call_target="tpu_custom_call" | custom-call | bytes 19200 | tf_op jit(solution)/shard_map/pallas_call | solution.py:61
  245.7 42.9 %shard_map.116.sum_ref = f32[72,256,128]{2,1,0:T(8,128)} custom-call(s32[3360]{0:T(1024)} %get-tuple-element.274.field_ref, s32[4]{0:T(128)} %get-tuple-element.275.count_ref, s32[1]{0:T(128)} %bitcast.15.at_ref, bf16[37,256,128]{2,1,0:T(8,128)(2,1)} %pad.4.x_ref, bf16[16,64,128,128]{3,2,1,0:T(8,128)(2,1)} %bitcast.59, f32[72,1,128]{2,1,0:T(1,128)} %bitcast.63), custom_call_target="tpu_custom_call" | custom-call | flops 17179869184 | bytes 33554432 | tf_op jit(solution)/shard_map/pallas_call | solution.py:227
  288.6 101.7 %all-gather.12.cloned.1.call-done = bf16[1200,128,128]{2,1,0:T(8,128)(2,1)} async-done(((bf16[75,128,128]{2,1,0:T(8,128)(2,1)}), bf16[1200,128,128]{2,1,0:T(8,128)(2,1)}) %all-gather.12.cloned.1.call-update) | async-done | bytes 39321616 | tf_op jit(solution)/shard_map/all_gather | solution.py:428
  390.2 20.0 %shard_map.117.x_ref = bf16[73,256,128]{2,1,0:T(8,128)(2,1)S(1)} custom-call(s32[2240]{0:T(1024)} %get-tuple-element.269.field_ref, s32[4]{0:T(128)} %get-tuple-element.270.count_ref, s32[1]{0:T(128)} %bitcast.15.at_ref, bf16[37,256,128]{2,1,0:T(8,128)(2,1)} %pad.4.x_ref, bf16[16,75,128,128]{3,2,1,0:T(8,128)(2,1)} %bitcast.40, ...), custom_call_target="tpu_custom_call" | custom-call | flops 9932111872 | bytes 19398656 | tf_op jit(solution)/shard_map/pallas_call | solution.py:227
  410.3 35.7 %shard_map.118 = (f32[36,256,128]{2,1,0:T(8,128)}, bf16[256,4608]{1,0:T(8,128)(2,1)}) custom-call(s32[3312]{0:T(1024)} %get-tuple-element.267.field_ref, s32[2]{0:T(128)} %get-tuple-element.268.count_ref, s32[1]{0:T(128)} %bitcast.15.at_ref, bf16[73,256,128]{2,1,0:T(8,128)(2,1)S(1)} %shard_map.117.x_ref, bf16[16,75,128,128]{3,2,1,0:T(8,128)(2,1)} %bitcast.41), custom_call_target="tpu_custom_call" | custom-call | flops 20132659200 | bytes 39321600 | tf_op jit(solution)/shard_map/pallas_call | solution.py:227
  452.6 14.5 %shard_map.112 = (s32[1568]{0:T(1024)}, s32[4]{0:T(128)}) custom-call(s32[528]{0:T(1024)} %reshape_reshape.12.row_ref, s32[528]{0:T(1024)} %select_n.157.col_ref), custom_call_target="tpu_custom_call" | custom-call | bytes 8448 | tf_op jit(solution)/shard_map/pallas_call | solution.py:61
  467.1 8.4 %collective-permute-done.5 = bf16[256,2304]{1,0:T(8,128)(2,1)S(1)} collective-permute-done((bf16[256,2304]{1,0:T(8,128)(2,1)S(1)}, bf16[256,2304]{1,0:T(8,128)(2,1)S(1)}, u32[]{:S(2)}, u32[]{:S(2)}) %collective-permute-start.5) | collective-permute-done | bytes 1179680 | tf_op jit(solution)/shard_map/ppermute | solution.py:533
  475.6 7.8 %all-gather.16.cloned.1.call-done = bf16[528,128,128]{2,1,0:T(8,128)(2,1)} async-done(((bf16[33,128,128]{2,1,0:T(8,128)(2,1)}), bf16[528,128,128]{2,1,0:T(8,128)(2,1)}) %all-gather.16.cloned.1.call-update) | async-done | bytes 17301520 | tf_op jit(solution)/shard_map/all_gather | solution.py:428
  483.4 17.6 %conditional.1 = (bf16[256,2304]{1,0:T(8,128)(2,1)S(1)}) conditional(s32[]{:T(128)} %convert_element_type.29, (s32[]{:T(128)}, s32[1568]{0:T(1024)}, s32[4]{0:T(128)}, bf16[73,256,128]{2,1,0:T(8,128)(2,1)}, bf16[16,33,128,128]{3,2,1,0:T(8,128)(2,1)}, /*index=5*/f32[36,256,128]{2,1,0:T(8,128)}, bf16[256,4608]{1,0:T(8,128)(2,1)}, ...), branch_computations={%region_6.7_spmd, %region_7.10_spmd} | conditional | flops 15571632128 | bytes 88065992 | solution.py:601
  483.4 17.6 %branch_0_fun.1 = bf16[256,2304]{1,0:T(8,128)(2,1)S(1)} custom-call(s32[1568]{0:T(1024)} %get-tuple-element.197.field_ref, s32[4]{0:T(128)} %get-tuple-element.198.count_ref, s32[1]{0:T(128)} %bitcast.at_ref, bf16[73,256,128]{2,1,0:T(8,128)(2,1)} %get-tuple-element.200.x_ref, bf16[16,33,128,128]{3,2,1,0:T(8,128)(2,1)} %get-tuple-element.201.w_ref, ...), custom_call_target="tpu_custom_call" | custom-call | flops 8858370048 | bytes 17301504 | tf_op jit(solution)/shard_map/cond/branch_0_fun/pallas_call | solution.py:227
  (125 shorter events, 29.4 us)
Async XLA Ops:
  6.5 4.8 copy-start.17
  6.5 4.8 copy-start.18
  6.5 239.1 %all-gather.14.cloned.1.call-start = ((), (), s32[]{:S(2)}) async-start(), calls=%async_computation.1 | async-start | bytes 35651584 | tf_op jit(solution)/shard_map/all_gather | solution.py:428
  9.7 70.4 %copy-start = (bf16[1,1,101,128,128]{4,3,2,1,0:T(8,128)(2,1)S(1)}, bf16[1,1,101,128,128]{4,3,2,1,0:T(8,128)(2,1)}, u32[]{:S(2)}) copy-start(bf16[1,1,101,128,128]{4,3,2,1,0:T(8,128)(2,1)} %param.22) | copy-start | bytes 9928708
  9.7 380.5 %all-gather.12.cloned.1.call-start = ((), (), s32[]{:S(2)}) async-start(), calls=%async_computation | async-start | bytes 41779200 | tf_op jit(solution)/shard_map/all_gather | solution.py:428
  76.9 60.4 %copy-start.20 = (s32[301]{0:T(512)}, s32[301]{0:T(512)S(1)}, u32[]{:S(2)}) copy-start(s32[301]{0:T(512)S(1)} %get-tuple-element.273) | copy-start | bytes 3616
  78.9 1.1 copy-start.1
  80.1 7.4 %copy-start.16 = (s32[76]{0:T(128)S(1)}, s32[76]{0:T(128)}, u32[]{:S(2)}) copy-start(s32[76]{0:T(128)} %get-tuple-element.272) | copy-start | bytes 916
  87.0 5.0 collective-permute-start.1
  90.1 3.1 copy-start.2
  92.0 1.2 copy-start.3
  101.1 21.5 %collective-permute-start.2 = (bf16[13,128,128]{2,1,0:T(8,128)(2,1)S(1)}, bf16[13,128,128]{2,1,0:T(8,128)(2,1)S(1)}, u32[]{:S(2)}, u32[]{:S(2)}) collective-permute-start(bf16[13,128,128]{2,1,0:T(8,128)(2,1)S(1)} %gather_fusion.2), channel_id=1, source_target_pairs={{0,4},{2,6},{4,0},{6,2},{8,12},{10,14},{12,8},{14,10},{16,20},{18,... | collective-permute-start | bytes 1277960 | tf_op jit(solution)/shard_map/ppermute | solution.py:453
  104.7 22.9 %collective-permute-start.3 = (bf16[10,128,128]{2,1,0:T(8,128)(2,1)S(1)}, bf16[10,128,128]{2,1,0:T(8,128)(2,1)S(1)}, u32[]{:S(2)}, u32[]{:S(2)}) collective-permute-start(bf16[10,128,128]{2,1,0:T(8,128)(2,1)S(1)} %gather_fusion.3), channel_id=1, source_target_pairs={{0,8},{2,10},{4,12},{6,14},{8,0},{10,2},{12,4},{14,6},{16,24},{18,... | collective-permute-start | bytes 983048 | tf_op jit(solution)/shard_map/ppermute | solution.py:453
  108.3 22.7 %collective-permute-start.4 = (bf16[8,128,128]{2,1,0:T(8,128)(2,1)S(1)}, bf16[8,128,128]{2,1,0:T(8,128)(2,1)S(1)}, u32[]{:S(2)}, u32[]{:S(2)}) collective-permute-start(bf16[8,128,128]{2,1,0:T(8,128)(2,1)S(1)} %gather_fusion.4), channel_id=1, source_target_pairs={{0,16},{2,18},{4,20},{6,22},{8,24},{10,26},{12,28},{14,30},{16,0},... | collective-permute-start | bytes 786440 | tf_op jit(solution)/shard_map/ppermute | solution.py:453
  137.2 5.0 copy-start.15
  137.2 5.7 %copy-start.14 = (s32[16]{0:T(128)S(1)}, s32[16]{0:T(128)}, u32[]{:S(2)}) copy-start(s32[16]{0:T(128)} %get-tuple-element.261) | copy-start | bytes 196
  137.2 13.8 %copy-start.8 = (s32[4816]{0:T(1024)S(1)}, s32[4816]{0:T(1024)}, u32[]{:S(2)}) copy-start(s32[4816]{0:T(1024)} %get-tuple-element.264) | copy-start | bytes 57796
  137.2 15.7 %copy-start.12 = (s32[16]{0:T(128)S(1)}, s32[16]{0:T(128)}, u32[]{:S(2)}) copy-start(s32[16]{0:T(128)} %get-tuple-element.284.left_ref) | copy-start | bytes 196
  137.2 346.2 %all-gather.16.cloned.1.call-start = ((), (), s32[]{:S(2)}) async-start(), calls=%async_computation.2 | async-start | bytes 18382848 | tf_op jit(solution)/shard_map/all_gather | solution.py:428
  151.2 2.5 copy-start.5
  157.2 1.3 copy-start.9
  157.2 1.3 copy-start.10
  410.3 35.8 %copy-start.4 = (bf16[73,256,128]{2,1,0:T(8,128)(2,1)}, bf16[73,256,128]{2,1,0:T(8,128)(2,1)S(1)}, u32[]{:S(2)}) copy-start(bf16[73,256,128]{2,1,0:T(8,128)(2,1)S(1)} %shard_map.117.x_ref) | copy-start | bytes 14352388
  410.3 38.8 %copy-start.11 = (f32[2304]{0:T(1024)S(1)}, f32[2304]{0:T(1024)}, u32[]{:S(2)}) copy-start(f32[2304]{0:T(1024)} %param.25) | copy-start | bytes 27652
  410.3 39.4 %copy-start.6 = (s32[16,301]{1,0:T(8,128)S(1)}, s32[16,301]{1,0:T(8,128)}, u32[]{:S(2)}) copy-start(s32[16,301]{1,0:T(8,128)} %copy-done.5) | copy-start | bytes 57796
  410.3 41.0 %copy-start.13 = (s32[3]{0:T(128)S(1)}, s32[3]{0:T(128)}, u32[]{:S(2)}) copy-start(s32[3]{0:T(128)} %pmax.7) | copy-start | bytes 40
  447.4 28.1 %collective-permute-start.5 = (bf16[256,2304]{1,0:T(8,128)(2,1)S(1)}, bf16[256,2304]{1,0:T(8,128)(2,1)S(1)}, u32[]{:S(2)}, u32[]{:S(2)}) collective-permute-start(bf16[256,2304]{1,0:T(8,128)(2,1)S(1)} %constant_dynamic-slice_fusion.1), channel_id=1, source_target_pairs={{0,1},{1,0},{2,3},{3,2},{4,5},{5,4},{6,7},{7,6},{8,9},{9,8},{10,11... | collective-permute-start | bytes 3538952 | tf_op jit(solution)/shard_map/ppermute | solution.py:533
  501.0 1.0 copy-start.21
Sparse Core Ops, SparseCore 0:
  9.9 183.4 all-gather.13
  194.9 195.2 all-gather.11
  391.8 91.5 all-gather.15
